TPU v7x, 32 devices: a whole 2x2x4 slice. The times are simulated.
32 devices in a mesh: section: 4 (over y, x), dp: 8 (over z, core).
Axes of the slice: x: 2, y: 2, z: 4, core: 2. Of those that a mesh axis runs over, the one named last changes fastest.
Arguments:
- small_images: bfloat16 [2, 8, 196, 768], P(None, 'dp'), may hold values from -6 to 6
- large_images: bfloat16 [2, 8, 576, 768], P(None, 'dp'), may hold values from -6 to 6
- small_upstream: bfloat16 [2, 8, 196, 768], P(None, 'dp'), may hold values from -6 to 6
- large_upstream: bfloat16 [2, 8, 576, 768], P(None, 'dp'), may hold values from -6 to 6
- small_keep: int32 [4, 2, 8, 2], P('section', None, 'dp'), may hold values 0 or 1
- large_keep: int32 [4, 2, 8, 2], P('section', None, 'dp'), may hold values 0 or 1
- small_in: bfloat16 [4, 196, 384], P('section'), may hold values from -0.4375 to 0.4375
- small_bias: float32 [4, 384], P('section'), may hold values from -1.5 to 1.5
- small_out: bfloat16 [4, 384, 196], P('section'), may hold values from -0.3125 to 0.3125
- small_shift: float32 [4, 196], P('section'), may hold values from -1.5 to 1.5
- large_in: bfloat16 [4, 576, 384], P('section'), may hold values from -0.25 to 0.25
- large_bias: float32 [4, 384], P('section'), may hold values from -1.5 to 1.5
- large_out: bfloat16 [4, 384, 576], P('section'), may hold values from -0.3125 to 0.3125
- large_shift: float32 [4, 576], P('section'), may hold values from -1.5 to 1.5
- channel_in: bfloat16 [4, 768, 3072], P('section'), may hold values from -0.21875 to 0.21875
- channel_bias: float32 [4, 3072], P('section'), may hold values from -1.5 to 1.5
- channel_out: bfloat16 [4, 3072, 768], P('section'), may hold values from -0.109375 to 0.109375
- channel_shift: float32 [4, 768], P('section'), may hold values from -1.5 to 1.5
- norm_gain: float32 [4, 2, 768], P('section'), may hold values from 0.5 to 1.5
- norm_shift: float32 [4, 2, 768], P('section'), may hold values from -1.5 to 1.5
Outputs:
- small_outputs: bfloat16 [4, 2, 8, 196, 768], P('section', None, 'dp')
- large_outputs: bfloat16 [4, 2, 8, 576, 768], P('section', None, 'dp')
- small_backward: bfloat16 [4, 2, 8, 196, 768], P('section', None, 'dp')
- large_backward: bfloat16 [4, 2, 8, 576, 768], P('section', None, 'dp')
- small_in_grad: float32 [4, 196, 384], P('section', None, 'dp')
- small_bias_grad: float32 [4, 384], P('section')
- small_out_grad: float32 [4, 384, 196], P('section', 'dp')
- small_shift_grad: float32 [4, 196], P('section')
- large_in_grad: float32 [4, 576, 384], P('section', None, 'dp')
- large_bias_grad: float32 [4, 384], P('section')
- large_out_grad: float32 [4, 384, 576], P('section', 'dp')
- large_shift_grad: float32 [4, 576], P('section')
- channel_in_grad: float32 [4, 768, 3072], P('section', 'dp')
- channel_bias_grad: float32 [4, 3072], P('section')
- channel_out_grad: float32 [4, 3072, 768], P('section', None, 'dp')
- channel_shift_grad: float32 [4, 768], P('section')
- norm_gain_grad: float32 [4, 2, 768], P('section')
- norm_shift_grad: float32 [4, 2, 768], P('section')
All inputs are finite; a program needn't handle non-finite values. No bound on the sum of `small_keep` or of `large_keep` on one device may be relied on, other than what follows from the above.
Results may differ from a plain program's by a relative error of at most 0.017.
Values may be sent and summed in bfloat16 or wider, within the bound.
A program may use at most 192 MiB of HBM per device.

v0:
```python
import jax
import jax.numpy as jnp
from jax import lax
from jax.sharding import PartitionSpec as P

EPSILON = 1e-06
ROOT_HALF = 0.7071067811865476
DENSITY = 0.3989422804014327


def shifted(x, axis, by):
    length = lax.axis_size(axis)
    pairs = [(i, i + by) for i in range(length) if 0 <= i + by < length]
    return lax.ppermute(x, axis, pairs)


def norm_forward(value, gain, shift):
    center = jnp.mean(value, axis=-1, keepdims=True)
    centred = value - center
    spread = jnp.mean(centred * centred, axis=-1, keepdims=True)
    scale = lax.rsqrt(spread + EPSILON)
    unit = centred * scale
    return (unit * gain + shift, unit, scale)


def norm_backward(grad_out, gain, unit, scale):
    scaled = grad_out * gain
    first = jnp.mean(scaled, axis=-1, keepdims=True)
    second = jnp.mean(scaled * unit, axis=-1, keepdims=True)
    grad_in = scale * (scaled - first - unit * second)
    return (grad_in, jnp.sum(grad_out * unit, axis=(0, 1)), jnp.sum(grad_out, axis=(0, 1)))


def gelu_pair(value):
    cdf = 0.5 * (1.0 + lax.erf(value * ROOT_HALF))
    return (value * cdf, cdf + value * DENSITY * jnp.exp(-0.5 * value * value))


def front(images, keep, token_set, shared):
    tok_in, tok_bias, tok_out, tok_shift = token_set
    chan_in, chan_bias, chan_out, chan_shift, gains, shifts = shared
    value = images.astype(jnp.float32)
    skips = keep.astype(jnp.float32)
    normed, unit_one, scale_one = norm_forward(value, gains[0], shifts[0])
    normed = normed.astype(jnp.bfloat16)
    pre = (
        jnp.einsum("sk,isd->ikd", tok_in, normed, preferred_element_type=jnp.float32)
        + tok_bias[None, :, None]
    )
    act, slope = gelu_pair(pre)
    hidden = act.astype(jnp.bfloat16)
    branch = (
        jnp.einsum("ks,ikd->isd", tok_out, hidden, preferred_element_type=jnp.float32)
        + tok_shift[None, :, None]
    )
    middle = value + skips[:, 0, None, None] * branch
    normed_two, unit_two, scale_two = norm_forward(middle, gains[1], shifts[1])
    normed_two = normed_two.astype(jnp.bfloat16)
    pre_two = (
        jnp.einsum("isd,dc->isc", normed_two, chan_in, preferred_element_type=jnp.float32)
        + chan_bias
    )
    act_two, slope_two = gelu_pair(pre_two)
    hidden_two = act_two.astype(jnp.bfloat16)
    return (
        skips,
        normed,
        unit_one,
        scale_one,
        slope,
        hidden,
        middle,
        normed_two,
        unit_two,
        scale_two,
        slope_two,
        hidden_two,
    )


def layer_output(images, keep, token_set, shared):
    kept = front(images, keep, token_set, shared)
    skips, middle, hidden_two = (kept[0], kept[6], kept[11])
    branch_two = (
        jnp.einsum("isc,cd->isd", hidden_two, shared[2], preferred_element_type=jnp.float32)
        + shared[3]
    )
    return (middle + skips[:, 1, None, None] * branch_two).astype(jnp.bfloat16)


def layer_grads(images, keep, token_set, shared, upstream):
    tok_in, tok_bias, tok_out, tok_shift = token_set
    chan_in, chan_bias, chan_out, chan_shift, gains, shifts = shared
    (
        skips,
        normed,
        unit_one,
        scale_one,
        slope,
        hidden,
        middle,
        normed_two,
        unit_two,
        scale_two,
        slope_two,
        hidden_two,
    ) = front(images, keep, token_set, shared)
    grad_out = upstream.astype(jnp.float32)
    grad_branch_two = (skips[:, 1, None, None] * grad_out).astype(jnp.bfloat16)
    chan_out_grad = jnp.einsum(
        "isc,isd->cd", hidden_two, grad_branch_two, preferred_element_type=jnp.float32
    )
    chan_shift_grad = jnp.sum(grad_branch_two.astype(jnp.float32), axis=(0, 1))
    grad_hidden_two = jnp.einsum(
        "isd,cd->isc", grad_branch_two, chan_out, preferred_element_type=jnp.float32
    )
    grad_pre_two = (grad_hidden_two * slope_two).astype(jnp.bfloat16)
    chan_in_grad = jnp.einsum(
        "isd,isc->dc", normed_two, grad_pre_two, preferred_element_type=jnp.float32
    )
    chan_bias_grad = jnp.sum(grad_pre_two.astype(jnp.float32), axis=(0, 1))
    grad_normed_two = jnp.einsum(
        "isc,dc->isd", grad_pre_two, chan_in, preferred_element_type=jnp.float32
    )
    back_two, gain_two, shift_two = norm_backward(grad_normed_two, gains[1], unit_two, scale_two)
    grad_middle = grad_out + back_two
    grad_branch = (skips[:, 0, None, None] * grad_middle).astype(jnp.bfloat16)
    tok_out_grad = jnp.einsum(
        "ikd,isd->ks", hidden, grad_branch, preferred_element_type=jnp.float32
    )
    tok_shift_grad = jnp.sum(grad_branch.astype(jnp.float32), axis=(0, 2))
    grad_hidden = jnp.einsum(
        "ks,isd->ikd", tok_out, grad_branch, preferred_element_type=jnp.float32
    )
    grad_pre = (grad_hidden * slope).astype(jnp.bfloat16)
    tok_in_grad = jnp.einsum("isd,ikd->sk", normed, grad_pre, preferred_element_type=jnp.float32)
    tok_bias_grad = jnp.sum(grad_pre.astype(jnp.float32), axis=(0, 2))
    grad_normed = jnp.einsum("sk,ikd->isd", tok_in, grad_pre, preferred_element_type=jnp.float32)
    back_one, gain_one, shift_one = norm_backward(grad_normed, gains[0], unit_one, scale_one)
    grad_in = (grad_middle + back_one).astype(jnp.bfloat16)
    token_terms = (tok_in_grad, tok_bias_grad, tok_out_grad, tok_shift_grad)
    shared_terms = (
        chan_in_grad,
        chan_bias_grad,
        chan_out_grad,
        chan_shift_grad,
        jnp.stack([gain_one, gain_two]),
        jnp.stack([shift_one, shift_two]),
    )
    return (grad_in, token_terms, shared_terms)


def pick(stack, index):
    return lax.dynamic_index_in_dim(stack, index, 0, keepdims=False)


def store(stack, index, value, valid):
    return lax.dynamic_update_index_in_dim(
        stack, jnp.where(valid, value, pick(stack, index)), index, 0
    )


def vector_terms(terms):
    return (terms[1], terms[3], terms[5], terms[7], terms[9], terms[11], terms[12], terms[13])


def local(
    small_images,
    large_images,
    small_upstream,
    large_upstream,
    small_keep,
    large_keep,
    small_in,
    small_bias,
    small_out,
    small_shift,
    large_in,
    large_bias,
    large_out,
    large_shift,
    channel_in,
    channel_bias,
    channel_out,
    channel_shift,
    norm_gain,
    norm_shift,
):
    sections = lax.axis_size("section")
    place = lax.axis_index("section")
    micro = small_images.shape[0]
    ticks = micro + sections - 1
    small_set = (small_in[0], small_bias[0], small_out[0], small_shift[0])
    large_set = (large_in[0], large_bias[0], large_out[0], large_shift[0])
    shared = (
        channel_in[0],
        channel_bias[0],
        channel_out[0],
        channel_shift[0],
        norm_gain[0],
        norm_shift[0],
    )
    weights_like = small_set + large_set + shared
    small_masks = small_keep[0]
    large_masks = large_keep[0]

    def forward_tick(tick, state):
        small_arriving, large_arriving, small_saved, large_saved, small_made, large_made = state
        offset = tick - place
        index = jnp.clip(offset, 0, micro - 1)
        valid = (offset >= 0) & (offset < micro)
        small_now = jnp.where(place == 0, pick(small_images, index), small_arriving)
        large_now = jnp.where(place == 0, pick(large_images, index), large_arriving)

        def forward_work(operands):
            return (
                layer_output(operands[0], pick(small_masks, index), small_set, shared),
                layer_output(operands[1], pick(large_masks, index), large_set, shared),
            )

        def forward_skipped(operands):
            return (jnp.zeros_like(operands[0]), jnp.zeros_like(operands[1]))

        small_result, large_result = lax.cond(
            valid, forward_work, forward_skipped, (small_now, large_now)
        )
        small_saved = store(small_saved, index, small_now, valid)
        large_saved = store(large_saved, index, large_now, valid)
        small_made = store(small_made, index, small_result, valid)
        large_made = store(large_made, index, large_result, valid)
        small_sent, large_sent = shifted((small_result, large_result), "section", 1)
        return (small_sent, large_sent, small_saved, large_saved, small_made, large_made)

    start = (
        jnp.zeros_like(small_images[0]),
        jnp.zeros_like(large_images[0]),
        jnp.zeros_like(small_images),
        jnp.zeros_like(large_images),
        jnp.zeros_like(small_images),
        jnp.zeros_like(large_images),
    )
    _, _, small_saved, large_saved, small_made, large_made = lax.fori_loop(
        0, ticks, forward_tick, start
    )
    start_totals = tuple((jnp.zeros(w.shape, jnp.float32) for w in weights_like))

    def backward_tick(tick, state):
        small_arriving, large_arriving, small_back, large_back, totals = state
        offset = tick - (sections - 1 - place)
        index = jnp.clip(offset, 0, micro - 1)
        valid = (offset >= 0) & (offset < micro)
        last = place == sections - 1
        small_grad_now = jnp.where(last, pick(small_upstream, index), small_arriving)
        large_grad_now = jnp.where(last, pick(large_upstream, index), large_arriving)

        def backward_work(operands):
            small_result, small_terms, small_common = layer_grads(
                pick(small_saved, index), pick(small_masks, index), small_set, shared, operands[0]
            )
            large_result, large_terms, large_common = layer_grads(
                pick(large_saved, index), pick(large_masks, index), large_set, shared, operands[1]
            )
            common = tuple((a + b for a, b in zip(small_common, large_common)))
            return (small_result, large_result, small_terms + large_terms + common)

        def backward_skipped(operands):
            return (
                jnp.zeros_like(operands[0]),
                jnp.zeros_like(operands[1]),
                jax.tree.map(jnp.zeros_like, start_totals),
            )

        small_result, large_result, terms = lax.cond(
            valid, backward_work, backward_skipped, (small_grad_now, large_grad_now)
        )
        totals = jax.tree.map(lambda a, b: a + b, totals, terms)
        small_back = store(small_back, index, small_result, valid)
        large_back = store(large_back, index, large_result, valid)
        small_sent, large_sent = shifted((small_result, large_result), "section", -1)
        return (small_sent, large_sent, small_back, large_back, totals)

    start = (
        jnp.zeros_like(small_images[0]),
        jnp.zeros_like(large_images[0]),
        jnp.zeros_like(small_images),
        jnp.zeros_like(large_images),
        start_totals,
    )
    _, _, small_back, large_back, totals = lax.fori_loop(0, ticks, backward_tick, start)
    matrices = (
        lax.psum_scatter(totals[0], "dp", scatter_dimension=1, tiled=True),
        lax.psum_scatter(totals[2], "dp", scatter_dimension=0, tiled=True),
        lax.psum_scatter(totals[4], "dp", scatter_dimension=1, tiled=True),
        lax.psum_scatter(totals[6], "dp", scatter_dimension=0, tiled=True),
        lax.psum_scatter(totals[8], "dp", scatter_dimension=0, tiled=True),
        lax.psum_scatter(totals[10], "dp", scatter_dimension=1, tiled=True),
    )
    vectors = vector_terms(totals)
    vectors = lax.psum(
        (
            vectors[0],
            vectors[1],
            vectors[2],
            vectors[3],
            vectors[4],
            vectors[5],
            vectors[6],
            vectors[7],
        ),
        "dp",
    )
    return (
        small_made[None],
        large_made[None],
        small_back[None],
        large_back[None],
        matrices[0][None],
        vectors[0][None],
        matrices[1][None],
        vectors[1][None],
        matrices[2][None],
        vectors[2][None],
        matrices[3][None],
        vectors[3][None],
        matrices[4][None],
        vectors[4][None],
        matrices[5][None],
        vectors[5][None],
        vectors[6][None],
        vectors[7][None],
    )


def solution(mesh):
    placed = (
        P(None, "dp", None, None),
        P(None, "dp", None, None),
        P(None, "dp", None, None),
        P(None, "dp", None, None),
        P("section", None, "dp", None),
        P("section", None, "dp", None),
        P("section", None, None),
        P("section", None),
        P("section", None, None),
        P("section", None),
        P("section", None, None),
        P("section", None),
        P("section", None, None),
        P("section", None),
        P("section", None, None),
        P("section", None),
        P("section", None, None),
        P("section", None),
        P("section", None, None),
        P("section", None, None),
    )
    return jax.shard_map(
        local,
        mesh=mesh,
        in_specs=placed,
        out_specs=(
            P("section", None, "dp", None, None),
            P("section", None, "dp", None, None),
            P("section", None, "dp", None, None),
            P("section", None, "dp", None, None),
            P("section", None, "dp"),
            P("section", None),
            P("section", "dp", None),
            P("section", None),
            P("section", None, "dp"),
            P("section", None),
            P("section", "dp", None),
            P("section", None),
            P("section", "dp", None),
            P("section", None),
            P("section", None, "dp"),
            P("section", None),
            P("section", None, None),
            P("section", None, None),
        ),
        check_vma=False,
    )
```

profile of v0, /device:TPU:0, one launch (start us, length us, event | category | flops | bytes accessed | tf_op | source)
XLA Modules:
  0.0 1410.6 jit_solution(6609578448434383403)
XLA Ops:
  17.5 321.5 %while.74 = (s32[]{:T(128)}, bf16[1,196,768]{2,1,0:T(8,128)(2,1)}, bf16[1,576,768]{2,1,0:T(8,128)(2,1)}, bf16[2,1,196,768]{3,2,1,0:T(8,128)(2,1)S(1)}, bf16[2,1,...) while((s32[]{:T(128)}, bf16[1,196,768]{2,1,0:T(8,128)(2,1)}, ...), condition=%wide.region_11.12_spmd, body=%wide.region_0.11_spmd.sunk | while | flops 8232936960 | bytes 54694468 | solution.py:242
  22.0 37.5 %conditional.5 = (bf16[1,196,768]{2,1,0:T(8,128)(2,1)}, bf16[1,576,768]{2,1,0:T(8,128)(2,1)S(1)}) conditional(s32[]{:T(128)} %convert_element_type.682, () %tuple.150, (bf16[1,196,768]{2,1,0:T(8,128)(2,1)}, s32[]{:T(128)}, s32[2,1,2]{2,1,0:T(1,128)}, f32[2,768]{1,0:T(2,128)S(1)}, f32[2,768]{1,0:T(2,128)S(1)}, /*index=5*/bf16[196,384]{1,0:T(8,128)(2,1)}, ...), branch_computations={%region_1.1_spmd, %region_2.10_spmd} | conditional | flops 8231158272 | bytes 32076742 | solution.py:224
  71.0 16.3 %collective-permute-done = bf16[1,196,768]{2,1,0:T(8,128)(2,1)} collective-permute-done((bf16[1,196,768]{2,1,0:T(8,128)(2,1)}, bf16[1,196,768]{2,1,0:T(8,128)(2,1)}, u32[]{:S(2)}, u32[]{:S(2)}) %collective-permute-start) | collective-permute-done | bytes 301088 | tf_op jit(solution)/shard_map/while/body/eval_jaxpr/ppermute | solution.py:14
  91.9 37.5 %conditional.5 = (bf16[1,196,768]{2,1,0:T(8,128)(2,1)}, bf16[1,576,768]{2,1,0:T(8,128)(2,1)S(1)}) conditional(s32[]{:T(128)} %convert_element_type.682, () %tuple.150, (bf16[1,196,768]{2,1,0:T(8,128)(2,1)}, s32[]{:T(128)}, s32[2,1,2]{2,1,0:T(1,128)}, f32[2,768]{1,0:T(2,128)S(1)}, f32[2,768]{1,0:T(2,128)S(1)}, /*index=5*/bf16[196,384]{1,0:T(8,128)(2,1)}, ...), branch_computations={%region_1.1_spmd, %region_2.10_spmd} | conditional | flops 8231158272 | bytes 32076742 | solution.py:224
  145.2 15.4 %collective-permute-done = bf16[1,196,768]{2,1,0:T(8,128)(2,1)} collective-permute-done((bf16[1,196,768]{2,1,0:T(8,128)(2,1)}, bf16[1,196,768]{2,1,0:T(8,128)(2,1)}, u32[]{:S(2)}, u32[]{:S(2)}) %collective-permute-start) | collective-permute-done | bytes 301088 | tf_op jit(solution)/shard_map/while/body/eval_jaxpr/ppermute | solution.py:14
  166.0 43.3 %collective-permute-start.1 = (bf16[1,576,768]{2,1,0:T(8,128)(2,1)S(1)}, bf16[1,576,768]{2,1,0:T(8,128)(2,1)}, u32[]{:S(2)}, u32[]{:S(2)}) collective-permute-start(bf16[1,576,768]{2,1,0:T(8,128)(2,1)S(1)} %get-tuple-element.2498), channel_id=1, source_target_pairs={{0,8},{8,16},{16,24},{1,9},{9,17},{17,25},{2,10},{10,18},{18,26},{... | collective-permute-start | bytes 2654216 | tf_op jit(solution)/shard_map/while/body/eval_jaxpr/ppermute | solution.py:14
  218.4 14.6 %collective-permute-done = bf16[1,196,768]{2,1,0:T(8,128)(2,1)} collective-permute-done((bf16[1,196,768]{2,1,0:T(8,128)(2,1)}, bf16[1,196,768]{2,1,0:T(8,128)(2,1)}, u32[]{:S(2)}, u32[]{:S(2)}) %collective-permute-start) | collective-permute-done | bytes 301088 | tf_op jit(solution)/shard_map/while/body/eval_jaxpr/ppermute | solution.py:14
  244.9 40.9 %collective-permute-start = (bf16[1,196,768]{2,1,0:T(8,128)(2,1)}, bf16[1,196,768]{2,1,0:T(8,128)(2,1)}, u32[]{:S(2)}, u32[]{:S(2)}) collective-permute-start(bf16[1,196,768]{2,1,0:T(8,128)(2,1)} %get-tuple-element.2497), channel_id=1, source_target_pairs={{0,8},{8,16},{16,24},{1,9},{9,17},{17,25},{2,10},{10,18},{18,26},{... | collective-permute-start | bytes 903176 | tf_op jit(solution)/shard_map/while/body/eval_jaxpr/ppermute | solution.py:14
  297.4 19.3 %collective-permute-start.1 = (bf16[1,576,768]{2,1,0:T(8,128)(2,1)S(1)}, bf16[1,576,768]{2,1,0:T(8,128)(2,1)}, u32[]{:S(2)}, u32[]{:S(2)}) collective-permute-start(bf16[1,576,768]{2,1,0:T(8,128)(2,1)S(1)} %get-tuple-element.2498), channel_id=1, source_target_pairs={{0,8},{8,16},{16,24},{1,9},{9,17},{17,25},{2,10},{10,18},{18,26},{... | collective-permute-start | bytes 2654216 | tf_op jit(solution)/shard_map/while/body/eval_jaxpr/ppermute | solution.py:14
  342.9 729.8 %while.75 = (s32[]{:T(128)}, bf16[1,196,768]{2,1,0:T(8,128)(2,1)}, bf16[1,576,768]{2,1,0:T(8,128)(2,1)}, bf16[2,1,196,768]{3,2,1,0:T(8,128)(2,1)}, bf16[2,1,576,...) while((s32[]{:T(128)}, bf16[1,196,768]{2,1,0:T(8,128)(2,1)}, ...), condition=%wide.region_47.48_spmd.clone, body=%wide.region_12.47_spmd.clone.sunk | while | flops 21070811136 | bytes 546415872 | solution.py:289
  344.6 23.4 %conditional.6 = (bf16[1,196,768]{2,1,0:T(8,128)(2,1)}, bf16[1,576,768]{2,1,0:T(8,128)(2,1)}, f32[196,384]{1,0:T(8,128)}, f32[384]{0:T(512)}, f32[384,196]{0,1:T...) conditional(s32[]{:T(128)} %convert_element_type.683, ...), branch_computations={%region_13.13_spmd, %region_14.46_spmd} | conditional | flops 21059577856 | bytes 420477280 | solution.py:273
  403.8 14.6 %collective-permute-done.2 = bf16[1,196,768]{2,1,0:T(8,128)(2,1)} collective-permute-done((bf16[1,196,768]{2,1,0:T(8,128)(2,1)}, bf16[1,196,768]{2,1,0:T(8,128)(2,1)}, u32[]{:S(2)}, u32[]{:S(2)}) %collective-permute-start.2) | collective-permute-done | bytes 301088 | tf_op jit(solution)/shard_map/while/body/eval_jaxpr/ppermute | solution.py:14
  420.3 23.4 %conditional.6 = (bf16[1,196,768]{2,1,0:T(8,128)(2,1)}, bf16[1,576,768]{2,1,0:T(8,128)(2,1)}, f32[196,384]{1,0:T(8,128)}, f32[384]{0:T(512)}, f32[384,196]{0,1:T...) conditional(s32[]{:T(128)} %convert_element_type.683, ...), branch_computations={%region_13.13_spmd, %region_14.46_spmd} | conditional | flops 21059577856 | bytes 420477280 | solution.py:273
  449.7 13.2 select_add_fusion.33
  487.2 23.4 %conditional.6 = (bf16[1,196,768]{2,1,0:T(8,128)(2,1)}, bf16[1,576,768]{2,1,0:T(8,128)(2,1)}, f32[196,384]{1,0:T(8,128)}, f32[384]{0:T(512)}, f32[384,196]{0,1:T...) conditional(s32[]{:T(128)} %convert_element_type.683, ...), branch_computations={%region_13.13_spmd, %region_14.46_spmd} | conditional | flops 21059577856 | bytes 420477280 | solution.py:273
  552.2 220.2 %collective-permute-done.2 = bf16[1,196,768]{2,1,0:T(8,128)(2,1)} collective-permute-done((bf16[1,196,768]{2,1,0:T(8,128)(2,1)}, bf16[1,196,768]{2,1,0:T(8,128)(2,1)}, u32[]{:S(2)}, u32[]{:S(2)}) %collective-permute-start.2) | collective-permute-done | bytes 301088 | tf_op jit(solution)/shard_map/while/body/eval_jaxpr/ppermute | solution.py:14
  774.3 102.7 %conditional.6 = (bf16[1,196,768]{2,1,0:T(8,128)(2,1)}, bf16[1,576,768]{2,1,0:T(8,128)(2,1)}, f32[196,384]{1,0:T(8,128)}, f32[384]{0:T(512)}, f32[384,196]{0,1:T...) conditional(s32[]{:T(128)} %convert_element_type.683, ...), branch_computations={%region_13.13_spmd, %region_14.46_spmd} | conditional | flops 21059577856 | bytes 420477280 | solution.py:273
  923.7 102.6 %conditional.6 = (bf16[1,196,768]{2,1,0:T(8,128)(2,1)}, bf16[1,576,768]{2,1,0:T(8,128)(2,1)}, f32[196,384]{1,0:T(8,128)}, f32[384]{0:T(512)}, f32[384,196]{0,1:T...) conditional(s32[]{:T(128)} %convert_element_type.683, ...), branch_computations={%region_13.13_spmd, %region_14.46_spmd} | conditional | flops 21059577856 | bytes 420477280 | solution.py:273
  1090.1 27.3 %all-reduce = (f32[1,384]{1,0:T(1,128)}, f32[1,196]{1,0:T(1,128)}, f32[1,384]{1,0:T(1,128)}, f32[1,576]{1,0:T(1,128)}, f32[1,3072]{1,0:T(1,128)}, /*index=5*/f32...) all-reduce(f32[1,384]{1,0:T(1,128)S(1)} %broadcast_in_dim.135, ...), channel_id=1, replica_groups=mesh['section'=4,'dp'=8] {'dp'}, use_global_device_ids=true, to_apply=%region_49.50 | all-reduce | flops 8452 | bytes 67616 | tf_op jit(solution)/shard_map/psum | solution.py:299
  1119.4 16.7 %reduce-scatter.9.cloned.1.call-done = f32[48,196]{1,0:T(8,128)} async-done(((f32[384,196]{1,0:T(8,128)}), f32[48,196]{1,0:T(8,128)}) %reduce-scatter.9.cloned.1.call-update) | async-done | bytes 37648 | tf_op jit(solution)/shard_map/reduce_scatter | solution.py:292
  1136.2 33.1 %reduce-scatter.11.cloned.1.call-done = f32[576,48]{0,1:T(8,128)} async-done(((f32[576,384]{0,1:T(8,128)}), f32[576,48]{0,1:T(8,128)}) %reduce-scatter.11.cloned.1.call-update) | async-done | bytes 110608 | tf_op jit(solution)/shard_map/reduce_scatter | solution.py:293
  1169.2 33.1 %reduce-scatter.13.cloned.1.call-done = f32[48,576]{1,0:T(8,128)} async-done(((f32[384,576]{1,0:T(8,128)}), f32[48,576]{1,0:T(8,128)}) %reduce-scatter.13.cloned.1.call-update) | async-done | bytes 110608 | tf_op jit(solution)/shard_map/reduce_scatter | solution.py:294
  1202.3 100.6 %reduce-scatter.17.cloned.1.call-done = f32[3072,96]{0,1:T(8,128)} async-done(((f32[3072,768]{0,1:T(8,128)}), f32[3072,96]{0,1:T(8,128)}) %reduce-scatter.17.cloned.1.call-update) | async-done | bytes 1179664 | tf_op jit(solution)/shard_map/reduce_scatter | solution.py:296
  1302.9 100.6 %reduce-scatter.15.cloned.1.call-done = f32[96,3072]{1,0:T(8,128)} async-done(((f32[768,3072]{1,0:T(8,128)}), f32[96,3072]{1,0:T(8,128)}) %reduce-scatter.15.cloned.1.call-update) | async-done | bytes 1179664 | tf_op jit(solution)/shard_map/reduce_scatter | solution.py:295
  (1127 shorter events, 666.7 us)
Async XLA Ops:
  7.2 1112.2 %reduce-scatter.7.cloned.1.call-start = ((), (), s32[]{:S(2)}) async-start(), calls=%async_computation.6 | async-start | bytes 442368 | tf_op jit(solution)/shard_map/reduce_scatter | solution.py:291
  59.6 27.8 %collective-permute-start.1 = (bf16[1,576,768]{2,1,0:T(8,128)(2,1)S(1)}, bf16[1,576,768]{2,1,0:T(8,128)(2,1)}, u32[]{:S(2)}, u32[]{:S(2)}) collective-permute-start(bf16[1,576,768]{2,1,0:T(8,128)(2,1)S(1)} %get-tuple-element.2498), channel_id=1, source_target_pairs={{0,8},{8,16},{16,24},{1,9},{9,17},{17,25},{2,10},{10,18},{18,26},{... | collective-permute-start | bytes 2654216 | tf_op jit(solution)/shard_map/while/body/eval_jaxpr/ppermute | solution.py:14
  61.8 25.5 %collective-permute-start = (bf16[1,196,768]{2,1,0:T(8,128)(2,1)}, bf16[1,196,768]{2,1,0:T(8,128)(2,1)}, u32[]{:S(2)}, u32[]{:S(2)}) collective-permute-start(bf16[1,196,768]{2,1,0:T(8,128)(2,1)} %get-tuple-element.2497), channel_id=1, source_target_pairs={{0,8},{8,16},{16,24},{1,9},{9,17},{17,25},{2,10},{10,18},{18,26},{... | collective-permute-start | bytes 903176 | tf_op jit(solution)/shard_map/while/body/eval_jaxpr/ppermute | solution.py:14
  129.4 31.2 %collective-permute-start.1 = (bf16[1,576,768]{2,1,0:T(8,128)(2,1)S(1)}, bf16[1,576,768]{2,1,0:T(8,128)(2,1)}, u32[]{:S(2)}, u32[]{:S(2)}) collective-permute-start(bf16[1,576,768]{2,1,0:T(8,128)(2,1)S(1)} %get-tuple-element.2498), channel_id=1, source_target_pairs={{0,8},{8,16},{16,24},{1,9},{9,17},{17,25},{2,10},{10,18},{18,26},{... | collective-permute-start | bytes 2654216 | tf_op jit(solution)/shard_map/while/body/eval_jaxpr/ppermute | solution.py:14
  135.9 24.7 %collective-permute-start = (bf16[1,196,768]{2,1,0:T(8,128)(2,1)}, bf16[1,196,768]{2,1,0:T(8,128)(2,1)}, u32[]{:S(2)}, u32[]{:S(2)}) collective-permute-start(bf16[1,196,768]{2,1,0:T(8,128)(2,1)} %get-tuple-element.2497), channel_id=1, source_target_pairs={{0,8},{8,16},{16,24},{1,9},{9,17},{17,25},{2,10},{10,18},{18,26},{... | collective-permute-start | bytes 903176 | tf_op jit(solution)/shard_map/while/body/eval_jaxpr/ppermute | solution.py:14
  166.0 67.1 %collective-permute-start.1 = (bf16[1,576,768]{2,1,0:T(8,128)(2,1)S(1)}, bf16[1,576,768]{2,1,0:T(8,128)(2,1)}, u32[]{:S(2)}, u32[]{:S(2)}) collective-permute-start(bf16[1,576,768]{2,1,0:T(8,128)(2,1)S(1)} %get-tuple-element.2498), channel_id=1, source_target_pairs={{0,8},{8,16},{16,24},{1,9},{9,17},{17,25},{2,10},{10,18},{18,26},{... | collective-permute-start | bytes 2654216 | tf_op jit(solution)/shard_map/while/body/eval_jaxpr/ppermute | solution.py:14
  238.4 53.7 %collective-permute-start.1 = (bf16[1,576,768]{2,1,0:T(8,128)(2,1)S(1)}, bf16[1,576,768]{2,1,0:T(8,128)(2,1)}, u32[]{:S(2)}, u32[]{:S(2)}) collective-permute-start(bf16[1,576,768]{2,1,0:T(8,128)(2,1)S(1)} %get-tuple-element.2498), channel_id=1, source_target_pairs={{0,8},{8,16},{16,24},{1,9},{9,17},{17,25},{2,10},{10,18},{18,26},{... | collective-permute-start | bytes 2654216 | tf_op jit(solution)/shard_map/while/body/eval_jaxpr/ppermute | solution.py:14
  244.9 47.1 %collective-permute-start = (bf16[1,196,768]{2,1,0:T(8,128)(2,1)}, bf16[1,196,768]{2,1,0:T(8,128)(2,1)}, u32[]{:S(2)}, u32[]{:S(2)}) collective-permute-start(bf16[1,196,768]{2,1,0:T(8,128)(2,1)} %get-tuple-element.2497), channel_id=1, source_target_pairs={{0,8},{8,16},{16,24},{1,9},{9,17},{17,25},{2,10},{10,18},{18,26},{... | collective-permute-start | bytes 903176 | tf_op jit(solution)/shard_map/while/body/eval_jaxpr/ppermute | solution.py:14
  297.4 41.6 %collective-permute-start.1 = (bf16[1,576,768]{2,1,0:T(8,128)(2,1)S(1)}, bf16[1,576,768]{2,1,0:T(8,128)(2,1)}, u32[]{:S(2)}, u32[]{:S(2)}) collective-permute-start(bf16[1,576,768]{2,1,0:T(8,128)(2,1)S(1)} %get-tuple-element.2498), channel_id=1, source_target_pairs={{0,8},{8,16},{16,24},{1,9},{9,17},{17,25},{2,10},{10,18},{18,26},{... | collective-permute-start | bytes 2654216 | tf_op jit(solution)/shard_map/while/body/eval_jaxpr/ppermute | solution.py:14
  368.0 50.4 %collective-permute-start.3 = (bf16[1,576,768]{2,1,0:T(8,128)(2,1)}, bf16[1,576,768]{2,1,0:T(8,128)(2,1)}, u32[]{:S(2)}, u32[]{:S(2)}) collective-permute-start(bf16[1,576,768]{2,1,0:T(8,128)(2,1)} %get-tuple-element.2542), channel_id=1, source_target_pairs={{8,0},{16,8},{24,16},{9,1},{17,9},{25,17},{10,2},{18,10},{26,18},{... | collective-permute-start | bytes 2654216 | tf_op jit(solution)/shard_map/while/body/eval_jaxpr/ppermute | solution.py:14
  369.4 49.0 %collective-permute-start.2 = (bf16[1,196,768]{2,1,0:T(8,128)(2,1)}, bf16[1,196,768]{2,1,0:T(8,128)(2,1)}, u32[]{:S(2)}, u32[]{:S(2)}) collective-permute-start(bf16[1,196,768]{2,1,0:T(8,128)(2,1)} %get-tuple-element.2541), channel_id=1, source_target_pairs={{8,0},{16,8},{24,16},{9,1},{17,9},{25,17},{10,2},{18,10},{26,18},{... | collective-permute-start | bytes 903176 | tf_op jit(solution)/shard_map/while/body/eval_jaxpr/ppermute | solution.py:14
  443.6 41.7 %collective-permute-start.3 = (bf16[1,576,768]{2,1,0:T(8,128)(2,1)}, bf16[1,576,768]{2,1,0:T(8,128)(2,1)}, u32[]{:S(2)}, u32[]{:S(2)}) collective-permute-start(bf16[1,576,768]{2,1,0:T(8,128)(2,1)} %get-tuple-element.2542), channel_id=1, source_target_pairs={{8,0},{16,8},{24,16},{9,1},{17,9},{25,17},{10,2},{18,10},{26,18},{... | collective-permute-start | bytes 2654216 | tf_op jit(solution)/shard_map/while/body/eval_jaxpr/ppermute | solution.py:14
  445.1 40.2 %collective-permute-start.2 = (bf16[1,196,768]{2,1,0:T(8,128)(2,1)}, bf16[1,196,768]{2,1,0:T(8,128)(2,1)}, u32[]{:S(2)}, u32[]{:S(2)}) collective-permute-start(bf16[1,196,768]{2,1,0:T(8,128)(2,1)} %get-tuple-element.2541), channel_id=1, source_target_pairs={{8,0},{16,8},{24,16},{9,1},{17,9},{25,17},{10,2},{18,10},{26,18},{... | collective-permute-start | bytes 903176 | tf_op jit(solution)/shard_map/while/body/eval_jaxpr/ppermute | solution.py:14
  510.6 261.9 %collective-permute-start.3 = (bf16[1,576,768]{2,1,0:T(8,128)(2,1)}, bf16[1,576,768]{2,1,0:T(8,128)(2,1)}, u32[]{:S(2)}, u32[]{:S(2)}) collective-permute-start(bf16[1,576,768]{2,1,0:T(8,128)(2,1)} %get-tuple-element.2542), channel_id=1, source_target_pairs={{8,0},{16,8},{24,16},{9,1},{17,9},{25,17},{10,2},{18,10},{26,18},{... | collective-permute-start | bytes 2654216 | tf_op jit(solution)/shard_map/while/body/eval_jaxpr/ppermute | solution.py:14
  512.0 260.4 %collective-permute-start.2 = (bf16[1,196,768]{2,1,0:T(8,128)(2,1)}, bf16[1,196,768]{2,1,0:T(8,128)(2,1)}, u32[]{:S(2)}, u32[]{:S(2)}) collective-permute-start(bf16[1,196,768]{2,1,0:T(8,128)(2,1)} %get-tuple-element.2541), channel_id=1, source_target_pairs={{8,0},{16,8},{24,16},{9,1},{17,9},{25,17},{10,2},{18,10},{26,18},{... | collective-permute-start | bytes 903176 | tf_op jit(solution)/shard_map/while/body/eval_jaxpr/ppermute | solution.py:14
  877.0 44.7 %collective-permute-start.3 = (bf16[1,576,768]{2,1,0:T(8,128)(2,1)}, bf16[1,576,768]{2,1,0:T(8,128)(2,1)}, u32[]{:S(2)}, u32[]{:S(2)}) collective-permute-start(bf16[1,576,768]{2,1,0:T(8,128)(2,1)} %get-tuple-element.2542), channel_id=1, source_target_pairs={{8,0},{16,8},{24,16},{9,1},{17,9},{25,17},{10,2},{18,10},{26,18},{... | collective-permute-start | bytes 2654216 | tf_op jit(solution)/shard_map/while/body/eval_jaxpr/ppermute | solution.py:14
  878.5 43.3 %collective-permute-start.2 = (bf16[1,196,768]{2,1,0:T(8,128)(2,1)}, bf16[1,196,768]{2,1,0:T(8,128)(2,1)}, u32[]{:S(2)}, u32[]{:S(2)}) collective-permute-start(bf16[1,196,768]{2,1,0:T(8,128)(2,1)} %get-tuple-element.2541), channel_id=1, source_target_pairs={{8,0},{16,8},{24,16},{9,1},{17,9},{25,17},{10,2},{18,10},{26,18},{... | collective-permute-start | bytes 903176 | tf_op jit(solution)/shard_map/while/body/eval_jaxpr/ppermute | solution.py:14
  1026.4 43.4 %collective-permute-start.3 = (bf16[1,576,768]{2,1,0:T(8,128)(2,1)}, bf16[1,576,768]{2,1,0:T(8,128)(2,1)}, u32[]{:S(2)}, u32[]{:S(2)}) collective-permute-start(bf16[1,576,768]{2,1,0:T(8,128)(2,1)} %get-tuple-element.2542), channel_id=1, source_target_pairs={{8,0},{16,8},{24,16},{9,1},{17,9},{25,17},{10,2},{18,10},{26,18},{... | collective-permute-start | bytes 2654216 | tf_op jit(solution)/shard_map/while/body/eval_jaxpr/ppermute | solution.py:14
  1027.8 41.9 %collective-permute-start.2 = (bf16[1,196,768]{2,1,0:T(8,128)(2,1)}, bf16[1,196,768]{2,1,0:T(8,128)(2,1)}, u32[]{:S(2)}, u32[]{:S(2)}) collective-permute-start(bf16[1,196,768]{2,1,0:T(8,128)(2,1)} %get-tuple-element.2541), channel_id=1, source_target_pairs={{8,0},{16,8},{24,16},{9,1},{17,9},{25,17},{10,2},{18,10},{26,18},{... | collective-permute-start | bytes 903176 | tf_op jit(solution)/shard_map/while/body/eval_jaxpr/ppermute | solution.py:14
  1074.8 61.4 %reduce-scatter.9.cloned.1.call-start = ((), (), s32[]{:S(2)}) async-start(), calls=%async_computation.7 | async-start | bytes 442368 | tf_op jit(solution)/shard_map/reduce_scatter | solution.py:292
  1076.7 92.5 %reduce-scatter.11.cloned.1.call-start = ((), (), s32[]{:S(2)}) async-start(), calls=%async_computation.8 | async-start | bytes 1105920 | tf_op jit(solution)/shard_map/reduce_scatter | solution.py:293
  1078.1 124.2 %reduce-scatter.13.cloned.1.call-start = ((), (), s32[]{:S(2)}) async-start(), calls=%async_computation.9 | async-start | bytes 1105920 | tf_op jit(solution)/shard_map/reduce_scatter | solution.py:294
  1079.5 223.4 %reduce-scatter.17.cloned.1.call-start = ((), (), s32[]{:S(2)}) async-start(), calls=%async_computation.11 | async-start | bytes 10616832 | tf_op jit(solution)/shard_map/reduce_scatter | solution.py:296
  1089.3 314.2 %reduce-scatter.15.cloned.1.call-start = ((), (), s32[]{:S(2)}) async-start(), calls=%async_computation.10 | async-start | bytes 10616832 | tf_op jit(solution)/shard_map/reduce_scatter | solution.py:295
  (332 other events, 3203.0 us)
Sparse Core Ops, SparseCore 0:
  1074.9 29.7 reduce-scatter.6
  1107.6 28.5 reduce-scatter.8
  1139.0 30.1 reduce-scatter.10
  1172.1 30.2 reduce-scatter.12
  1205.1 97.7 reduce-scatter.16
  1305.6 97.8 reduce-scatter.14
where the time goes:
time: 1430 us; the launch traced here: 1410 us
  waiting for transfers between devices  578 us (40%)
  other arithmetic  280 us (20%)
  matrix products  199 us (14%)
  starting transfers between devices  145 us (10%)
  local copies, waits for them, and re-layouts  144 us (10%)
  blocking collectives  27.3 us (2%)
  loops' own time  22.4 us (2%)
  between operations  14.7 us (1%)
    ppermute x20, waiting for transfers between devices, shifted(): return lax.ppermute(x, axis, pairs)  294 us
    add x60, other arithmetic, backward_tick(): totals = jax.tree.map(lambda a, b: a + b, totals, terms)  171 us
    ppermute x20, starting transfers between devices, shifted(): return lax.ppermute(x, axis, pairs)  144 us
    reduce_scatter x1, waiting for transfers between devices, local(): lax.psum_scatter(totals[8], 'dp', scatter_dimension=0, tiled=True)  101 us
    reduce_scatter x1, waiting for transfers between devices, local(): lax.psum_scatter(totals[10], 'dp', scatter_dimension=1, tiled=True)  101 us
    another operation x64, local copies, waits for them, and re-layouts  67.5 us
    dynamic_update_slice x30, other arithmetic, store(): lax.dynamic_update_index_in_dim(stack, jnp.where(valid, value, pick(stack...  38.4 us
    dot_general x4, matrix products, layer_output(): jnp.einsum('isc,cd->isd', hidden_two, shared[2], preferred_element_type=j...  38.4 us
  transfers between devices with their start and end apart: 26, of which 12 were waited for; matrix products, arithmetic and copies ran while one was open for 17% of the time, Pallas kernels for 0%

commit v1 on v0

v1 whole, which is shorter than its diff:
```python
import functools

import jax
import jax.numpy as jnp
from jax import lax
from jax.experimental import pallas as pl
from jax.experimental.pallas import tpu as pltpu
from jax.sharding import PartitionSpec as P

MESH = pl.DeviceIdType.MESH
F32 = jnp.float32
BF16 = jnp.bfloat16
EPSILON = 1e-06
DENSITY = 0.3989422804014327
ROWS = 144
COLS = 256
WIDE = 512


def up_to(value, step):
    return -(-value // step) * step


def mm(a, b, ca, cb):
    return lax.dot_general(a, b, (((ca,), (cb,)), ((), ())), preferred_element_type=F32)


def gelu_pair(v):
    cdf = 0.5 + 0.5 * lax.erf(v * 0.7071067811865476)
    bell = jnp.exp2((v * v) * (-0.5 * 1.4426950408889634))
    return v * cdf, cdf + (v * DENSITY) * bell


def groups(x):
    return x.reshape(x.shape[0] // 8, 8, x.shape[1]).sum(0)


def kernel(
    dims,
    small_images,
    large_images,
    small_upstream,
    large_upstream,
    small_keep,
    large_keep,
    small_in,
    small_bias,
    small_out,
    small_shift,
    large_in,
    large_bias,
    large_out,
    large_shift,
    channel_in,
    channel_bias,
    channel_out,
    channel_shift,
    norm_gain,
    norm_shift,
    small_made,
    large_made,
    small_back,
    large_back,
    chan_a,
    chan_b,
    tok_l,
    tok_s,
    vec_out,
    win,
    wout,
    hid,
    slope,
    xin,
    up,
    n1,
    n2,
    u2,
    r2,
    gb1,
    stage,
    h1,
    sl1,
    lgin,
    lgin_t,
    lgout,
    lgout_t,
    sgin,
    sgin_t,
    sgout,
    sgout_t,
    turned,
    lbcol,
    lscol,
    sbcol,
    sscol,
    mid,
    acc,
    raw_a,
    raw_b,
    sums,
    wsem,
    isem,
    usem,
    ysem,
    gsem,
    fs,
    fr,
    bs,
    br,
    sibs,
    rights,
    lefts,
    outsem,
    vsem,
    ready,
    tl,
    ts,
    vecs,
):
    sections, n, ps, pl_, pp, d, ds_, dc, dp, fused = dims
    place = lax.axis_index("section")
    ahead = lax.rem(place + 1, sections)
    behind = lax.rem(place + sections - 1, sections)
    last = place // (sections - 1)
    first_rows = n * pl_
    half = pl_ // 2
    line = dp // 2 if fused else 1
    rank = lax.axis_index("dp")
    z = rank // 2
    core = rank % 2
    sibling = rank + 1 - 2 * core

    def weight_copies():
        pairs = (
            (large_in, lgin),
            (large_out, lgout_t),
            (small_in, raw_a.at[0, :, pl.ds(0, ds_)]),
            (small_out, raw_a.at[0, :, pl.ds(ds_, ds_)]),
            (channel_in, win),
            (channel_out, wout),
        )
        return [pltpu.make_async_copy(a, b, wsem.at[k]) for k, (a, b) in enumerate(pairs)]

    def large_copy(src, dst, sem, i):
        return pltpu.make_async_copy(src.at[i], dst.at[pl.ds(pl.multiple_of(i * pl_, 64), pl_)], sem.at[i])

    def small_copy(src, dst, sem, j):
        return pltpu.make_async_copy(src.at[j], dst.at[j], sem.at[n + j])

    copies = weight_copies()

    @pl.when(place == 0)
    def _():
        for i in range(n):
            large_copy(large_images, xin, isem, i).start()

    for c in copies:
        c.start()

    @pl.when(last == 1)
    def _():
        for i in range(n):
            large_copy(large_upstream, up, usem, i).start()
        for j in range(n):
            small_copy(small_upstream, raw_b, usem, j).start()

    barrier = pltpu.get_barrier_semaphore()

    @pl.when(place > 0)
    def _():
        pl.semaphore_signal(barrier, inc=1, device_id={"section": behind}, device_id_type=MESH)

    @pl.when(place < sections - 1)
    def _():
        pl.semaphore_signal(barrier, inc=1, device_id={"section": ahead}, device_id_type=MESH)

    peers = (place + sections - 2) // (sections - 1) + 1 - last
    if fused:
        pl.semaphore_signal(barrier, inc=1, device_id={"dp": sibling}, device_id_type=MESH)
        for k in range(1, line):
            pl.semaphore_signal(barrier, inc=1, device_id={"dp": (rank + 2 * k) % dp}, device_id_type=MESH)
        peers = peers + line
    pl.semaphore_wait(barrier, peers)

    def column(row, dst):
        width = up_to(dst.shape[0], 128)
        sums[0:1, 0:width] = jnp.zeros((1, width), F32)
        sums[0:1, 0 : row.shape[1]] = row
        dst[...] = jnp.transpose(jnp.broadcast_to(sums[0:1, 0:width], (128, width)))[0 : dst.shape[0]]

    column(large_bias[...], lbcol)
    column(large_shift[...], lscol)
    column(small_bias[...], sbcol)
    column(small_shift[...], sscol)
    sums[...] = jnp.zeros(sums.shape, F32)
    for c in copies[:4]:
        c.wait()
    for k, padded in enumerate((sgin, sgout_t)):
        padded[...] = jnp.zeros(padded.shape, BF16)
        padded[0:ps, :] = raw_a[0, :, k * ds_ : (k + 1) * ds_]

    @pl.when(place == 0)
    def _():
        for j in range(n):
            small_copy(small_images, raw_a, isem, j).start()

    lgin_t[...] = jnp.transpose(lgin[...])
    lgout[...] = jnp.transpose(lgout_t[...])
    sgin_t[...] = jnp.transpose(sgin[...])
    sgout[...] = jnp.transpose(sgout_t[...])

    gains = norm_gain[...]
    shifts = norm_shift[...]

    def ahead_copy(rows, size, k):
        return pltpu.make_async_remote_copy(
            src_ref=stage.at[pl.ds(rows, size)],
            dst_ref=xin.at[pl.ds(rows, size)],
            send_sem=fs.at[k],
            recv_sem=fr.at[k],
            device_id={"section": ahead},
            device_id_type=MESH,
        )

    def behind_copy(rows, size, k):
        return pltpu.make_async_remote_copy(
            src_ref=stage.at[pl.ds(rows, size)],
            dst_ref=up.at[pl.ds(rows, size)],
            send_sem=bs.at[k],
            recv_sem=br.at[k],
            device_id={"section": behind},
            device_id_type=MESH,
        )

    class Unit:
        def __init__(self, large, i):
            self.large = large
            self.i = i
            self.rows = pl_ if large else pp
            self.blocks = 2 if large else 1
            self.size = self.rows // self.blocks
            self.some = ROWS if large else pp
            self.base = pl.multiple_of(i * pl_, 64) if large else pl.multiple_of(first_rows + i * pp, 16)
            self.head = pl.multiple_of((i if large else n + i) * ds_, 128)
            self.heads = pl.ds(self.head, ds_)
            self.slot = i * 2 if large else 2 * n + i
            self.gin, self.gin_t = (lgin, lgin_t) if large else (sgin, sgin_t)
            self.gout, self.gout_t = (lgout, lgout_t) if large else (sgout, sgout_t)
            self.bcol, self.scol = (lbcol, lscol) if large else (sbcol, sscol)
            self.mask = large_keep if large else small_keep

        def at(self, offset, size):
            return pl.ds(pl.multiple_of(self.base + offset, 16), size)

        def keep(self, which):
            return self.mask[self.i, which].astype(F32)

        def out_copy(self, which, b):
            sem = (ysem, gsem)[which].at[self.slot + b]
            if self.large:
                dst = (large_made, large_back)[which]
                return pltpu.make_async_copy(
                    stage.at[self.at(b * half, half)], dst.at[self.i, pl.ds(b * half, half)], sem
                )
            src = (raw_a, raw_b)[which]
            dst = (small_made, small_back)[which]
            return pltpu.make_async_copy(src.at[self.i], dst.at[self.i], sem)

    units = 2 * n

    def unit_at(which):
        return (which + core) % 2, which // 2

    def forward(unit, step):
        @pl.when(place == 0)
        def _():
            if unit.large:
                large_copy(large_images, xin, isem, unit.i).wait()
            else:
                small_copy(small_images, raw_a, isem, unit.i).wait()
                xin[unit.at(0, pp)] = jnp.zeros((pp, d), BF16)
                xin[unit.at(0, ps)] = raw_a[unit.i]

        def norm_one(r):
            rows = unit.at(r * unit.some, unit.some)
            x = xin[rows].astype(F32)
            x = x - jnp.mean(x, axis=1, keepdims=True)
            s = lax.rsqrt(jnp.mean(x * x, axis=1, keepdims=True) + EPSILON)
            n1[rows] = (x * s * gains[0:1] + shifts[0:1]).astype(BF16)

        steps = unit.size // unit.some
        for b in range(unit.blocks):

            @pl.when(place > 0)
            def _(b=b):
                ahead_copy(unit.base + b * unit.size, unit.size, unit.slot + b).wait_recv()

            for r in range(b * steps, (b + 1) * steps):
                norm_one(r)
        rows = unit.at(0, unit.rows)
        keep_one = unit.keep(0)
        keep_two = unit.keep(1)
        for c in range(0, d, COLS):
            pre = mm(unit.gin_t[...], n1[rows, c : c + COLS], 1, 0) + unit.bcol[:, 0:1]
            act, slp = gelu_pair(pre)
            h1[unit.heads, c : c + COLS] = act.astype(BF16)
            sl1[unit.heads, c : c + COLS] = slp.astype(BF16)
        for c in range(0, d, COLS):
            branch = mm(unit.gout_t[...], h1[unit.heads, c : c + COLS], 1, 0) + unit.scol[:, 0:1]
            mid[0 : unit.rows, c : c + COLS] = xin[rows, c : c + COLS].astype(F32) + keep_one * branch

        def norm_two(r):
            rows = unit.at(r * unit.some, unit.some)
            x = mid[r * unit.some : (r + 1) * unit.some]
            x = x - jnp.mean(x, axis=1, keepdims=True)
            s = lax.rsqrt(jnp.mean(x * x, axis=1, keepdims=True) + EPSILON)
            x = x * s
            u2[rows] = x.astype(BF16)
            r2[rows] = jnp.broadcast_to(s, (unit.some, 128))
            n2[rows] = (x * gains[1:2] + shifts[1:2]).astype(BF16)

        for r in range(unit.rows // unit.some):
            norm_two(r)

        @pl.when(step == 0)
        def _():
            for c in copies[4:]:
                c.wait()

        for b in range(unit.blocks):
            size = unit.size
            rows = unit.at(b * size, size)
            here = slice(b * size, (b + 1) * size)
            total = channel_shift[...]
            parts = [slice(c, c + WIDE) for c in range(0, dc, WIDE)]
            ahead_of = mm(n2[rows], win[:, parts[0]], 1, 0)
            for c, cols in enumerate(parts):
                pre = ahead_of + channel_bias[:, cols]
                if c + 1 < len(parts):
                    ahead_of = mm(n2[rows], win[:, parts[c + 1]], 1, 0)
                act, slp = gelu_pair(pre)
                act = act.astype(BF16)
                hid[rows, cols] = act
                slope[rows, cols] = slp.astype(BF16)
                total = total + mm(act, wout[cols, :], 1, 0)
            y = (mid[here] + keep_two * total).astype(BF16)
            stage[rows] = y
            if not unit.large:
                raw_a[unit.i] = y[0:ps]

            @pl.when(place < sections - 1)
            def _(b=b, size=size):
                ahead_copy(unit.base + b * size, size, unit.slot + b).start()

            unit.out_copy(0, b).start()

    def backward(unit):
        @pl.when(last == 1)
        def _():
            if unit.large:
                large_copy(large_upstream, up, usem, unit.i).wait()
            else:
                small_copy(small_upstream, raw_b, usem, unit.i).wait()
                up[unit.at(0, pp)] = jnp.zeros((pp, d), BF16)
                up[unit.at(0, ps)] = raw_b[unit.i]

        keep_one = unit.keep(0)
        keep_two = unit.keep(1)
        size = unit.size
        for b in range(unit.blocks):
            rows = unit.at(b * size, size)
            here = slice(b * size, (b + 1) * size)

            @pl.when(place < sections - 1)
            def _(b=b):
                ahead_copy(unit.base + b * size, size, unit.slot + b).wait_send()

            unit.out_copy(0, b).wait()

            @pl.when(last == 0)
            def _(b=b):
                behind_copy(unit.base + b * size, size, unit.slot + b).wait_recv()

            stage[rows] = up[rows] * keep_two.astype(BF16)

            parts = [slice(c, c + WIDE) for c in range(0, dc, WIDE)]
            total = None
            ahead_of = mm(stage[rows], wout[parts[0], :], 1, 1)
            for c, cols in enumerate(parts):
                grad = ahead_of
                if c + 1 < len(parts):
                    ahead_of = mm(stage[rows], wout[parts[c + 1], :], 1, 1)
                grad = (grad * slope[rows, cols].astype(F32)).astype(BF16)
                slope[rows, cols] = grad
                term = mm(grad, win[:, cols], 1, 1)
                total = term if total is None else total + term
            acc[here] = total

        def norm_two(r):
            offset = r * unit.some
            rows = unit.at(offset, unit.some)
            local = slice(offset, offset + unit.some)
            h = acc[local]
            u = u2[rows].astype(F32)
            s = r2[rows][:, 0:1]
            g = up[rows].astype(F32)
            q = h * gains[1:2]
            first = jnp.mean(q, axis=1, keepdims=True)
            second = jnp.mean(q * u, axis=1, keepdims=True)
            g_mid = g + s * (q - first - u * second)
            mid[local] = g_mid
            gb1[rows] = (keep_one * g_mid).astype(BF16)
            up[rows] = (keep_two * g).astype(BF16)
            return groups(h * u), groups(h)

        parts = [norm_two(r) for r in range(unit.rows // unit.some)]
        sums[8:16, 0:d] += sum(p[0] for p in parts)
        sums[24:32, 0:d] += sum(p[1] for p in parts)
        rows = unit.at(0, unit.rows)
        for c in range(0, d, COLS):
            grad = mm(unit.gout[...], gb1[rows, c : c + COLS], 1, 0)
            grad = (grad * sl1[unit.heads, c : c + COLS].astype(F32)).astype(BF16)
            sl1[unit.heads, c : c + COLS] = grad
        for c in range(0, d, COLS):
            acc[0 : unit.rows, c : c + COLS] = mm(unit.gin[...], sl1[unit.heads, c : c + COLS], 1, 0)

        def norm_one(r):
            offset = r * unit.some
            rows = unit.at(offset, unit.some)
            local = slice(offset, offset + unit.some)
            x = xin[rows].astype(F32)
            x = x - jnp.mean(x, axis=1, keepdims=True)
            s = lax.rsqrt(jnp.mean(x * x, axis=1, keepdims=True) + EPSILON)
            u = x * s
            h = acc[local]
            q = h * gains[0:1]
            first = jnp.mean(q, axis=1, keepdims=True)
            second = jnp.mean(q * u, axis=1, keepdims=True)
            stage[rows] = (mid[local] + s * (q - first - u * second)).astype(BF16)
            return groups(h * u), groups(h)

        steps = size // unit.some
        for b in range(unit.blocks):
            parts = [norm_one(r) for r in range(b * steps, (b + 1) * steps)]
            sums[0:8, 0:d] += sum(p[0] for p in parts)
            sums[16:24, 0:d] += sum(p[1] for p in parts)
            if not unit.large:
                raw_b[unit.i] = stage[unit.at(0, ps)]

            @pl.when(place > 0)
            def _(b=b):
                behind_copy(unit.base + b * size, size, unit.slot + b).start()

            unit.out_copy(1, b).start()

    piece = d // dp
    tok_piece = ds_ // dp

    def turn(src):
        def some(rows, size):
            value = jnp.transpose(src[pl.ds(rows, size)])
            if not fused:
                turned[:, pl.ds(rows, size)] = value
                return
            for b in range(dp):
                at = ((b % 2) * line + b // 2) * piece
                turned[at : at + piece, pl.ds(rows, size)] = value[b * piece : (b + 1) * piece]

        def full(r, carry):
            some(pl.multiple_of(r * 128, 128), 128)
            return carry

        whole = src.shape[0] // 128
        lax.fori_loop(0, whole, full, 0)
        if src.shape[0] % 128:
            some(whole * 128, src.shape[0] % 128)


    def step(t, carry):
        back = (1 - last) * (t // units) + last * (t % 2)
        which = (1 - last) * (t % units) + last * (t // 2)
        small, i = unit_at(which)

        @pl.when(t == 2 * units - 1)
        def _():
            turn(n2)

        @pl.when((back == 0) & (small == 0))
        def _():
            forward(Unit(True, i), t)

        @pl.when((back == 0) & (small == 1))
        def _():
            forward(Unit(False, i), t)

        @pl.when((back == 1) & (small == 0))
        def _():
            backward(Unit(True, i))

        @pl.when((back == 1) & (small == 1))
        def _():
            backward(Unit(False, i))

        return carry

    lax.fori_loop(0, 2 * units, step, 0)

    total = hid.shape[0]
    chunks = dc // d
    kinds = (chunks, chunks, 1, 1)
    first_of = (0, chunks, 2 * chunks, 2 * chunks + 1)
    count = sum(kinds)
    large_width, small_width = up_to(pl_, 128), up_to(pp, 128)
    widths = (d, d, large_width, small_width)
    own = line
    across = line + 1

    def columns(kind, k):
        if kind < 2:
            return pl.ds(pl.multiple_of(k * d, 128), d)
        return pl.ds(0, widths[kind])

    def own_rows(kind):
        return ((slope, 0), (hid, 0), (up, 0), (up, d))[kind]

    def weight_product(kind, k):
        src = (slope, hid)[kind]

        def part(j, carry):
            cols = pl.ds(pl.multiple_of(k * d + j * COLS, COLS), COLS)
            if kind == 0:
                bias = mm(jnp.ones((8, total), BF16), src[:, cols], 1, 0)[0:1]
                vecs[own, pl.ds(k, 1), pl.ds(pl.multiple_of(j * COLS, COLS), COLS)] = bias
            src[0:d, cols] = mm(turned[...], src[:, cols], 1, 0).astype(BF16)
            return carry

        lax.fori_loop(0, d // COLS, part, 0)

    def token_product(large):
        unit_rows = pl_ if large else pp
        ones_d = jnp.ones((8, d), BF16)
        out_grad = in_grad = bias = shift = None
        for k in range(n):
            base = k * pl_ if large else first_rows + k * pp
            head = k * ds_ if large else (n + k) * ds_
            g = gb1[base : base + unit_rows]
            x = n1[base : base + unit_rows]
            h = h1[head : head + ds_]
            p = sl1[head : head + ds_]
            terms = (mm(p, x, 1, 1), mm(h, g, 1, 1), mm(ones_d, p, 1, 1), mm(ones_d, g, 1, 1))
            if k == 0:
                in_grad, out_grad, bias, shift = terms
            else:
                in_grad, out_grad, bias, shift = in_grad + terms[0], out_grad + terms[1], bias + terms[2], shift + terms[3]
        src, base = own_rows(2 if large else 3)
        for at, value in ((0, in_grad), (1, out_grad)):
            value = value.astype(BF16)
            if not fused:
                src[base + at * ds_ : base + (at + 1) * ds_, 0:unit_rows] = value
                continue
            for b in range(dp):
                to = base + ((b % 2) * line + b // 2) * piece + at * tok_piece
                src[to : to + tok_piece, 0:unit_rows] = value[b * tok_piece : (b + 1) * tok_piece]
        row = chunks + 5 + (0 if large else 2)
        vecs[own, row : row + 1, 0:ds_] = bias[0:1]
        vecs[own, row + 1 : row + 2, 0:unit_rows] = shift[0:1]

    def product(kind, k):
        if kind < 2:
            if kind == 1:

                @pl.when(k == 0)
                def _():
                    turn(up)
                    vecs[own, chunks : chunks + 1] = mm(jnp.ones((8, total), BF16), up[...], 1, 0)[0:1]
                    for j in range(4):
                        vecs[own, chunks + 1 + j : chunks + 2 + j] = jnp.sum(sums[8 * j : 8 * j + 8], axis=0, keepdims=True)

            weight_product(kind, k)
        else:
            token_product(kind == 2)

    def ways(step_of):
        def at(c, valid=True):
            for kind in range(4):
                low, high = first_of[kind], first_of[kind] + kinds[kind]

                @pl.when((c >= low) & (c < high) & valid)
                def _(kind=kind, low=low):
                    step_of(kind, c - low)

        return at

    vecs[own] = jnp.zeros(vecs.shape[1:], F32)
    if not fused:

        def whole_copies(kind, k):
            src, base = own_rows(kind)
            if kind < 2:
                cols = columns(kind, k)
                dst = (chan_a, chan_b)[kind]
                return [pltpu.make_async_copy(src.at[pl.ds(0, d), cols], dst.at[:, cols], outsem.at[first_of[kind] + k])]
            cols = pl.ds(0, widths[kind])
            dst = (tok_l, tok_s)[kind - 2]
            return [pltpu.make_async_copy(src.at[pl.ds(base, d), cols], dst, outsem.at[first_of[kind]])]

        def one(kind, k):
            product(kind, k)
            for c in whole_copies(kind, k):
                c.start()

        def finish(kind, k):
            for c in whole_copies(kind, k):
                c.wait()

        def run(c, carry):
            ways(one)(c)
            return carry

        def end(c, carry):
            ways(finish)(c)
            return carry

        lax.fori_loop(0, count, run, 0)
        lax.fori_loop(0, count, end, 0)
        vec_out[...] = vecs[own]
    else:
        rightward, leftward = (rank + 2) % dp, (rank + dp - 2) % dp

        def mine(kind, k, to, core_of=core):
            src, base = own_rows(kind)
            return src.at[pl.ds(pl.multiple_of(base + (core_of * line + to) * piece, 16), piece), columns(kind, k)]

        def crossing(kind, k, rows, size):
            ref, base = ((win, 0), (win, d // 2), (wout, 3 * d), (wout, 3 * d + d // 2))[kind]
            return ref.at[pl.ds(pl.multiple_of(base + rows, 16), size), columns(kind, k)]

        def from_left(kind, k, to):
            ref, base = ((wout, 0), (wout, chunks * (line - 1)), (n2, 0), (n2, line - 1))[kind]
            rows = (base + k * (line - 1) + to - 1) * piece
            return ref.at[pl.ds(pl.multiple_of(rows, 16), piece), pl.ds(0, widths[kind])]

        def from_right(kind, k, to):
            ref, base = ((xin, 0), (u2, 0), (n2, 2 * (line - 1)), (n2, 3 * (line - 1)))[kind]
            rows = (base + k * (line - 1) + to) * piece
            return ref.at[pl.ds(pl.multiple_of(rows, 16), piece), pl.ds(0, widths[kind])]

        def sem_of(kind, k, to):
            return (first_of[kind] + k) * line + to

        def cross_copy(kind, k):
            src, base = own_rows(kind)
            rows = pl.ds(pl.multiple_of(base + (1 - core) * line * piece, 16), line * piece)
            c = first_of[kind] + k
            return pltpu.make_async_remote_copy(
                src_ref=src.at[rows, columns(kind, k)],
                dst_ref=crossing(kind, k, 0, line * piece),
                send_sem=sibs.at[0, c],
                recv_sem=sibs.at[1, c],
                device_id={"dp": sibling},
                device_id_type=MESH,
            )

        def right_copy(kind, k, to):
            return pltpu.make_async_remote_copy(
                src_ref=mine(kind, k, to),
                dst_ref=from_left(kind, k, to),
                send_sem=rights.at[0, sem_of(kind, k, to)],
                recv_sem=rights.at[1, sem_of(kind, k, to)],
                device_id={"dp": rightward},
                device_id_type=MESH,
            )

        def left_copy(kind, k, to):
            return pltpu.make_async_remote_copy(
                src_ref=mine(kind, k, to),
                dst_ref=from_right(kind, k, to),
                send_sem=lefts.at[0, sem_of(kind, k, to)],
                recv_sem=lefts.at[1, sem_of(kind, k, to)],
                device_id={"dp": leftward},
                device_id_type=MESH,
            )

        def chip_sum(kind, k, to):
            return mine(kind, k, to)[...].astype(F32) + crossing(kind, k, to * piece, piece)[...].astype(F32)

        def flow_right(kind, k):
            def one(j, carry):
                to = line - 1 - j

                @pl.when(z == 0)
                def _():
                    mine(kind, k, to)[...] = chip_sum(kind, k, to).astype(BF16)

                @pl.when(z > 0)
                def _():
                    right_copy(kind, k, to).wait_recv()
                    value = chip_sum(kind, k, to) + from_left(kind, k, to)[...].astype(F32)
                    mine(kind, k, to)[...] = value.astype(BF16)

                right_copy(kind, k, to).start()
                return carry

            lax.fori_loop(0, line - 1 - z, one, 0)

        def flow_left(kind, k):
            def one(to, carry):
                @pl.when(z == line - 1)
                def _():
                    mine(kind, k, to)[...] = chip_sum(kind, k, to).astype(BF16)

                @pl.when(z < line - 1)
                def _():
                    left_copy(kind, k, to).wait_recv()
                    value = chip_sum(kind, k, to) + from_right(kind, k, to)[...].astype(F32)
                    mine(kind, k, to)[...] = value.astype(BF16)

                left_copy(kind, k, to).start()
                return carry

            lax.fori_loop(0, z, one, 0)

        def out_stage(kind, k):
            if kind == 0:
                return mid.at[pl.ds(pl.multiple_of(k * piece, 16), piece)]
            if kind == 1:
                return acc.at[pl.ds(pl.multiple_of(k * piece, 16), piece)]
            return (tl, ts)[kind - 2]

        def out_copies(kind, k):
            c = first_of[kind] + k
            if kind < 2:
                dst = (chan_a, chan_b)[kind].at[:, columns(kind, k)]
            else:
                dst = (tok_l, tok_s)[kind - 2]
            return pltpu.make_async_copy(out_stage(kind, k), dst, outsem.at[c])

        def gather(kind, k):
            width = (d, d, pl_, ps)[kind]
            dst = out_stage(kind, k)
            dst[...] = chip_sum(kind, k, z)[:, 0:width]

            @pl.when(z > 0)
            def _():
                right_copy(kind, k, z).wait_recv()
                dst[...] += from_left(kind, k, z)[...].astype(F32)[:, 0:width]

            @pl.when(z < line - 1)
            def _():
                left_copy(kind, k, z).wait_recv()
                dst[...] += from_right(kind, k, z)[...].astype(F32)[:, 0:width]

            out_copies(kind, k).start()

        def vec_cross():
            return pltpu.make_async_remote_copy(
                src_ref=vecs.at[own],
                dst_ref=vecs.at[across],
                send_sem=vsem.at[0, 0],
                recv_sem=vsem.at[1, 0],
                device_id={"dp": sibling},
                device_id_type=MESH,
            )

        def vec_copy(k):
            return pltpu.make_async_remote_copy(
                src_ref=vecs.at[z],
                dst_ref=vecs.at[z],
                send_sem=vsem.at[0, k],
                recv_sem=vsem.at[1, k],
                device_id={"dp": (rank + 2 * k) % dp},
                device_id_type=MESH,
            )

        def first(kind, k):
            product(kind, k)
            if kind == 0:

                @pl.when(k == 0)
                def _():
                    pl.semaphore_wait(ready.at[0], 1)

                    @pl.when(z < line - 1)
                    def _():
                        pl.semaphore_wait(ready.at[1], 1)

                    @pl.when(z > 0)
                    def _():
                        pl.semaphore_wait(ready.at[2], 1)

            cross_copy(kind, k).start()

        def crossed(kind, k):
            cross_copy(kind, k).wait_recv()

        def finish(kind, k):
            cross_copy(kind, k).wait_send()
            out_copies(kind, k).wait()

            def right(j, carry):
                right_copy(kind, k, line - 1 - j).wait_send()
                return carry

            def left(to, carry):
                left_copy(kind, k, to).wait_send()
                return carry

            lax.fori_loop(0, line - 1 - z, right, 0)
            lax.fori_loop(0, z, left, 0)

        pl.semaphore_signal(ready.at[0], inc=1, device_id={"dp": sibling}, device_id_type=MESH)

        @pl.when(z > 0)
        def _():
            pl.semaphore_signal(ready.at[1], inc=1, device_id={"dp": leftward}, device_id_type=MESH)

        @pl.when(z < line - 1)
        def _():
            pl.semaphore_signal(ready.at[2], inc=1, device_id={"dp": rightward}, device_id_type=MESH)

        def run(c, carry):

            ways(crossed)(c - 1)
            ways(flow_right)(c - 1 - z, z < line - 1)
            ways(flow_left)(c - line + z, z > 0)
            ways(first)(c)

            @pl.when(c == count)
            def _():
                vec_cross().start()

            @pl.when(c == count + 1)
            def _():
                vec_cross().wait()
                vecs[z] = vecs[own] + vecs[across]
                for k in range(1, line):
                    vec_copy(k).start()

            ways(gather)(c - line - 1)
            return carry

        lax.fori_loop(0, count + line + 1, run, 0)

        def end(c, carry):
            ways(finish)(c)
            return carry

        lax.fori_loop(0, count, end, 0)
        for k in range(1, line):
            vec_copy(k).wait()
        value = vecs[0]
        for k in range(1, line):
            value = value + vecs[k]
        vec_out[...] = value

    for i in range(2 * n):
        unit = Unit(i < n, i % n)
        for b in range(unit.blocks):
            unit.out_copy(1, b).wait()

            @pl.when(place > 0)
            def _(b=b, unit=unit):
                behind_copy(unit.base + b * unit.size, unit.size, unit.slot + b).wait_send()


def finish_kernel(tok_piece, d, chunks, tok_l, tok_s, vec, *outs):
    for k, src in enumerate((tok_l, tok_s)):
        outs[2 * k][...] = src[0:tok_piece]
        outs[2 * k + 1][...] = src[tok_piece:]
    for k in range(chunks):
        outs[4][:, k * d : (k + 1) * d] = vec[k : k + 1]
    at = chunks
    for out in outs[5:]:
        rows, width = out.shape
        out[...] = vec[at : at + rows, 0:width]
        at += rows


def local(
    small_images,
    large_images,
    small_upstream,
    large_upstream,
    small_keep,
    large_keep,
    small_in,
    small_bias,
    small_out,
    small_shift,
    large_in,
    large_bias,
    large_out,
    large_shift,
    channel_in,
    channel_bias,
    channel_out,
    channel_shift,
    norm_gain,
    norm_shift,
):
    sections = lax.axis_size("section")
    micro, imgs, ps, d = small_images.shape
    pl_ = large_images.shape[2]
    n = micro * imgs
    ds_ = small_in.shape[2]
    dc = channel_in.shape[2]
    pp = up_to(ps, 16)
    rows = n * (pl_ + pp)
    small_width, large_width = up_to(pp, 128), up_to(pl_, 128)
    dp = lax.axis_size("dp")
    piece, tok_piece = d // dp, ds_ // dp
    fused = d % (16 * dp) == 0 and ds_ % (16 * dp) == 0 and dc == 4 * d and d == 2 * ds_ and 2 * dp * piece <= rows
    dims = (sections, n, ps, pl_, pp, d, ds_, dc, dp, fused)
    chunks = dc // d
    line = dp // 2 if fused else 1
    count = 2 * chunks + 2
    vec_rows = up_to(chunks + 9, 8)
    any_ = pl.BlockSpec(memory_space=pl.ANY)
    vmem = pl.BlockSpec(memory_space=pltpu.VMEM)
    smem = pl.BlockSpec(memory_space=pltpu.SMEM)
    block = max(pl_, n * pp)
    blocks = 2 * n + n
    scratch = [
        pltpu.VMEM((d, dc), BF16),
        pltpu.VMEM((dc, d), BF16),
        pltpu.VMEM((rows, dc), BF16),
        pltpu.VMEM((rows, dc), BF16),
        pltpu.VMEM((rows, d), BF16),
        pltpu.VMEM((rows, d), BF16),
        pltpu.VMEM((rows, d), BF16),
        pltpu.VMEM((rows, d), BF16),
        pltpu.VMEM((rows, d), BF16),
        pltpu.VMEM((rows, 128), F32),
        pltpu.VMEM((rows, d), BF16),
        pltpu.VMEM((rows, d), BF16),
        pltpu.VMEM((2 * n * ds_, d), BF16),
        pltpu.VMEM((2 * n * ds_, d), BF16),
        pltpu.VMEM((pl_, ds_), BF16),
        pltpu.VMEM((ds_, pl_), BF16),
        pltpu.VMEM((ds_, pl_), BF16),
        pltpu.VMEM((pl_, ds_), BF16),
        pltpu.VMEM((pp, ds_), BF16),
        pltpu.VMEM((ds_, pp), BF16),
        pltpu.VMEM((ds_, pp), BF16),
        pltpu.VMEM((pp, ds_), BF16),
        pltpu.VMEM((d, rows), BF16),
        pltpu.VMEM((ds_, 128), F32),
        pltpu.VMEM((pl_, 128), F32),
        pltpu.VMEM((ds_, 128), F32),
        pltpu.VMEM((pp, 128), F32),
        pltpu.VMEM((block, d), F32),
        pltpu.VMEM((block, d), F32),
        pltpu.VMEM((n, ps, d), BF16),
        pltpu.VMEM((n, ps, d), BF16),
        pltpu.VMEM((32, d), F32),
        pltpu.SemaphoreType.DMA((6,)),
        pltpu.SemaphoreType.DMA((2 * n,)),
        pltpu.SemaphoreType.DMA((2 * n,)),
        pltpu.SemaphoreType.DMA((blocks,)),
        pltpu.SemaphoreType.DMA((blocks,)),
        pltpu.SemaphoreType.DMA((blocks,)),
        pltpu.SemaphoreType.DMA((blocks,)),
        pltpu.SemaphoreType.DMA((blocks,)),
        pltpu.SemaphoreType.DMA((blocks,)),
        pltpu.SemaphoreType.DMA((2, count)),
        pltpu.SemaphoreType.DMA((2, count * line)),
        pltpu.SemaphoreType.DMA((2, count * line)),
        pltpu.SemaphoreType.DMA((count,)),
        pltpu.SemaphoreType.DMA((2, line)),
        pltpu.SemaphoreType.REGULAR((3,)),
        pltpu.VMEM((2 * tok_piece, pl_), F32),
        pltpu.VMEM((2 * tok_piece, ps), F32),
        pltpu.VMEM((line + 2, vec_rows, d), F32),
    ]
    if fused:
        reduced = (
            jax.ShapeDtypeStruct((piece, dc), F32),
            jax.ShapeDtypeStruct((piece, dc), F32),
            jax.ShapeDtypeStruct((2 * tok_piece, pl_), F32),
            jax.ShapeDtypeStruct((2 * tok_piece, ps), F32),
        )
    else:
        reduced = (
            jax.ShapeDtypeStruct((d, dc), BF16),
            jax.ShapeDtypeStruct((d, dc), BF16),
            jax.ShapeDtypeStruct((d, large_width), BF16),
            jax.ShapeDtypeStruct((d, small_width), BF16),
        )
    outs = (
        jax.ShapeDtypeStruct((n, ps, d), BF16),
        jax.ShapeDtypeStruct((n, pl_, d), BF16),
        jax.ShapeDtypeStruct((n, ps, d), BF16),
        jax.ShapeDtypeStruct((n, pl_, d), BF16),
        *reduced,
        jax.ShapeDtypeStruct((vec_rows, d), F32),
    )
    made_s, made_l, back_s, back_l, chan_a, chan_b, tok_l, tok_s, vec = pl.pallas_call(
        functools.partial(kernel, dims),
        out_shape=outs,
        in_specs=[any_] * 4
        + [smem] * 2
        + [any_, vmem, any_, vmem] * 2
        + [any_, vmem, any_, vmem]
        + [vmem, vmem],
        out_specs=(any_,) * 8 + (vmem,),
        scratch_shapes=scratch,
        compiler_params=pltpu.CompilerParams(
            collective_id=0, has_side_effects=True, vmem_limit_bytes=65400 * 1024
        ),
        cost_estimate=pl.CostEstimate(flops=50 * 10**9, bytes_accessed=40 * 10**6, transcendentals=10**7),
    )(
        small_images.reshape(n, ps, d),
        large_images.reshape(n, pl_, d),
        small_upstream.reshape(n, ps, d),
        large_upstream.reshape(n, pl_, d),
        small_keep.reshape(n, 2),
        large_keep.reshape(n, 2),
        small_in[0],
        small_bias,
        small_out[0].T,
        small_shift,
        large_in[0],
        large_bias,
        large_out[0].T,
        large_shift,
        channel_in[0],
        channel_bias,
        channel_out[0],
        channel_shift,
        norm_gain[0],
        norm_shift[0],
    )
    if fused:
        final = [jax.ShapeDtypeStruct((tok_piece, width), F32) for width in (pl_, pl_, ps, ps)]
        final += [
            jax.ShapeDtypeStruct(shape, F32)
            for shape in ((1, dc), (1, d), (2, d), (2, d), (1, ds_), (1, pl_), (1, ds_), (1, ps))
        ]
        lin, lout, sin, sout, cbias, cshift, gain, shift, lbias, lshift, sbias, sshift = pl.pallas_call(
            functools.partial(finish_kernel, tok_piece, d, chunks),
            out_shape=final,
            in_specs=[vmem] * 3,
            out_specs=[vmem] * 12,
        )(tok_l, tok_s, vec)
    else:
        chan_a, chan_b = (lax.psum_scatter(x, "dp", scatter_dimension=0, tiled=True).astype(F32) for x in (chan_a, chan_b))
        tok = jnp.concatenate([tok_l, tok_s], axis=1).reshape(2, ds_, large_width + small_width)
        tok = lax.psum_scatter(tok, "dp", scatter_dimension=1, tiled=True).astype(F32)
        lin, lout, sin, sout = tok[0, :, 0:pl_], tok[1, :, 0:pl_], tok[0, :, large_width:], tok[1, :, large_width:]
        sin, sout = sin[:, 0:ps], sout[:, 0:ps]
        vec = lax.psum(vec, "dp")
        at = chunks
        cbias, cshift = vec[0:at].reshape(1, dc), vec[at : at + 1]
        gain, shift = vec[at + 1 : at + 3], vec[at + 3 : at + 5]
        lbias, lshift = vec[at + 5 : at + 6, 0:ds_], vec[at + 6 : at + 7, 0:pl_]
        sbias, sshift = vec[at + 7 : at + 8, 0:ds_], vec[at + 8 : at + 9, 0:ps]
    return (
        made_s.reshape(1, micro, imgs, ps, d),
        made_l.reshape(1, micro, imgs, pl_, d),
        back_s.reshape(1, micro, imgs, ps, d),
        back_l.reshape(1, micro, imgs, pl_, d),
        sin.T[None],
        sbias,
        sout[None],
        sshift,
        lin.T[None],
        lbias,
        lout[None],
        lshift,
        chan_a[None],
        cbias,
        chan_b.T[None],
        cshift,
        gain[None],
        shift[None],
    )


def solution(mesh):
    placed = (
        (P(None, "dp", None, None),) * 4
        + (P("section", None, "dp", None),) * 2
        + (P("section", None, None), P("section", None)) * 6
        + (P("section", None, None),) * 2
    )
    outs = (
        (P("section", None, "dp", None, None),) * 4
        + (P("section", None, "dp"), P("section", None), P("section", "dp", None), P("section", None)) * 2
        + (P("section", "dp", None), P("section", None), P("section", None, "dp"), P("section", None))
        + (P("section", None, None),) * 2
    )
    return jax.shard_map(local, mesh=mesh, in_specs=placed, out_specs=outs, check_vma=False)
```

time: 1430 us -> 311 us (0.22); the launches traced: 1410 us -> 310 us
  waiting for transfers between devices: 578 us -> 0 us
  Pallas kernels: 0 us -> 296 us
  other arithmetic: 280 us -> 0 us
  matrix products: 199 us -> 0 us
  starting transfers between devices: 145 us -> 0 us
  local copies, waits for them, and re-layouts: 144 us -> 13.8 us
  blocking collectives: 27.3 us -> 0 us
  loops' own time: 22.4 us -> 0 us
    pallas_call x0 -> x2, Pallas kernels: none -> 296 us  [the longest x1 294 us: local(): pl.pallas_call(functools.partial(kernel, dims), out_shape=outs, in_specs=...]
    ppermute x20 -> x0, waiting for transfers between devices: 294 us -> none  [shifted(): return lax.ppermute(x, axis, pairs)]
    reduce_scatter x6 -> x0, waiting for transfers between devices: 284 us -> none  [the longest x1 101 us: local(): lax.psum_scatter(totals[8], 'dp', scatter_dimension=0, tiled=True)]
    dot_general x52 -> x0, matrix products: 199 us -> none  [the longest x4 38.4 us: layer_output(): jnp.einsum('isc,cd->isd', hidden_two, shared[2], preferred_element_type=j...]
    add x68 -> x0, other arithmetic: 175 us -> none  [the longest x60 171 us: backward_tick(): totals = jax.tree.map(lambda a, b: a + b, totals, terms)]
    ppermute x20 -> x0, starting transfers between devices: 144 us -> none  [shifted(): return lax.ppermute(x, axis, pairs)]
    another operation x80 -> x0, local copies, waits for them, and re-layouts: 67.6 us -> none
    reduce_sum x36 -> x0, other arithmetic: 45.7 us -> none  [the longest x4 12.6 us: layer_grads(): chan_shift_grad = jnp.sum(grad_branch_two.astype(jnp.float32), axis=(0, 1))]
  transfers between devices with their start and end apart: 26 -> 0, of which waited for: 12 -> 0; matrix products, arithmetic and copies ran while one was open for 17% -> 0% of each run, Pallas kernels for 0% -> 0%
where the time goes in v1:
time: 311 us; the launch traced here: 310 us
  Pallas kernels  296 us (95%)
  local copies, waits for them, and re-layouts  13.8 us (4%)
    pallas_call x1, Pallas kernels, local(): pl.pallas_call(functools.partial(kernel, dims), out_shape=outs, in_specs=...  294 us
    unnamed x14, local copies, waits for them, and re-layouts  11.4 us

profile of v1, /device:TPU:0, one launch (start us, length us, event | category | flops | bytes accessed | tf_op | source)
XLA Modules:
  0.0 310.5 jit_solution(7939054100952066845)
XLA Ops:
  0.7 2.4 copy_bitcast_fusion
  3.1 294.1 %shard_map.331 = (bf16[2,196,768]{2,1,0:T(8,128)(2,1)}, bf16[2,576,768]{2,1,0:T(8,128)(2,1)}, bf16[2,196,768]{2,1,0:T(8,128)(2,1)}, bf16[2,576,768]{2,1,0:T(8,12...) custom-call(bf16[2,196,768]{2,1,0:T(8,128)(2,1)} %get-tuple-element., ...), custom_call_target="tpu_custom_call" | custom-call | flops 49999998976 | bytes 40000000 | tf_op jit(solution)/shard_map/pallas_call | solution.py:997
  297.1 0.0 copy-start.1
  297.1 1.9 shard_map.332
  299.0 2.4 copy.40
  301.4 2.4 copy.42
  303.7 0.0 copy-done.1
  303.7 0.0 copy-start
  303.7 1.2 copy.50
  304.9 0.9 copy-done
  305.8 0.0 copy-start.3
  305.8 1.2 copy.51
  307.1 0.7 copy-done.3
  307.8 0.0 copy-start.2
  307.8 1.0 copy.52
  308.8 0.7 copy-done.2
  309.5 1.0 copy.53
Async XLA Ops:
  297.1 6.6 %copy-start.1 = (bf16[2,576,768]{2,1,0:T(8,128)(2,1)S(1)}, bf16[2,576,768]{2,1,0:T(8,128)(2,1)}, u32[]{:S(2)}) copy-start(bf16[2,576,768]{2,1,0:T(8,128)(2,1)} %get-tuple-element.40) | copy-start | bytes 5308420
  303.7 2.1 copy-start
  305.8 1.9 copy-start.3
  307.8 1.7 copy-start.2

commit v2 on v1

--- a/solution.py
+++ b/solution.py
@@ -113,11 +113,14 @@
     outsem,
     vsem,
     ready,
+    lent,
     tl,
     ts,
     vecs,
+    paired,
+    pairs,
 ):
-    sections, n, ps, pl_, pp, d, ds_, dc, dp, fused = dims
+    sections, n, ps, pl_, pp, d, ds_, dc, dp, fused, shared = dims
     place = lax.axis_index("section")
     ahead = lax.rem(place + 1, sections)
     behind = lax.rem(place + sections - 1, sections)
@@ -129,6 +132,9 @@
     z = rank // 2
     core = rank % 2
     sibling = rank + 1 - 2 * core
+    partner = (place + sections // 2) % sections
+    giver = place < sections // 2
+    taker = place >= sections // 2
 
     def weight_copies():
         pairs = (
@@ -179,7 +185,8 @@
         pl.semaphore_signal(barrier, inc=1, device_id={"dp": sibling}, device_id_type=MESH)
         for k in range(1, line):
             pl.semaphore_signal(barrier, inc=1, device_id={"dp": (rank + 2 * k) % dp}, device_id_type=MESH)
-        peers = peers + line
+        pl.semaphore_signal(barrier, inc=1, device_id={"section": partner}, device_id_type=MESH)
+        peers = peers + line + 1
     pl.semaphore_wait(barrier, peers)
 
     def column(row, dst):
@@ -352,7 +359,8 @@
             def _(b=b, size=size):
                 ahead_copy(unit.base + b * size, size, unit.slot + b).start()
 
-            unit.out_copy(0, b).start()
+            if unit.large or not fused:
+                unit.out_copy(0, b).start()
 
     def backward(unit):
         @pl.when(last == 1)
@@ -375,7 +383,8 @@
             def _(b=b):
                 ahead_copy(unit.base + b * size, size, unit.slot + b).wait_send()
 
-            unit.out_copy(0, b).wait()
+            if unit.large or not fused:
+                unit.out_copy(0, b).wait()
 
             @pl.when(last == 0)
             def _(b=b):
@@ -451,7 +460,8 @@
             def _(b=b):
                 behind_copy(unit.base + b * size, size, unit.slot + b).start()
 
-            unit.out_copy(1, b).start()
+            if unit.large or not fused:
+                unit.out_copy(1, b).start()
 
     piece = d // dp
     tok_piece = ds_ // dp
@@ -507,11 +517,11 @@
 
     total = hid.shape[0]
     chunks = dc // d
-    kinds = (chunks, chunks, 1, 1)
-    first_of = (0, chunks, 2 * chunks, 2 * chunks + 1)
-    count = sum(kinds)
+    count = 2 * chunks + 2
+    kinds = (chunks, chunks, 1, 1, shared)
+    first_of = (0, chunks + 2, chunks, chunks + 1, count + 1)
     large_width, small_width = up_to(pl_, 128), up_to(pp, 128)
-    widths = (d, d, large_width, small_width)
+    widths = (d, d, large_width, small_width, d)
     own = line
     across = line + 1
 
@@ -566,26 +576,27 @@
         vecs[own, row + 1 : row + 2, 0:unit_rows] = shift[0:1]
 
     def product(kind, k):
+        if kind == 2:
+            turn(up)
+            vecs[own, chunks : chunks + 1] = mm(jnp.ones((8, total), BF16), up[...], 1, 0)[0:1]
+            for j in range(4):
+                vecs[own, chunks + 1 + j : chunks + 2 + j] = jnp.sum(sums[8 * j : 8 * j + 8], axis=0, keepdims=True)
         if kind < 2:
-            if kind == 1:
-
-                @pl.when(k == 0)
-                def _():
-                    turn(up)
-                    vecs[own, chunks : chunks + 1] = mm(jnp.ones((8, total), BF16), up[...], 1, 0)[0:1]
-                    for j in range(4):
-                        vecs[own, chunks + 1 + j : chunks + 2 + j] = jnp.sum(sums[8 * j : 8 * j + 8], axis=0, keepdims=True)
-
             weight_product(kind, k)
         else:
             token_product(kind == 2)
 
-    def ways(step_of):
+    def ways(step_of, kept=False):
         def at(c, valid=True):
-            for kind in range(4):
+            for kind in range(5 if fused else 4):
                 low, high = first_of[kind], first_of[kind] + kinds[kind]
-
-                @pl.when((c >= low) & (c < high) & valid)
+                here = (c >= low) & (c < high) & valid
+                if kind == 4:
+                    here = here & taker
+                if kind == 0 and kept:
+                    here = here & (taker | (c < 1) | (c > shared))
+
+                @pl.when(here)
                 def _(kind=kind, low=low):
                     step_of(kind, c - low)
 
@@ -627,26 +638,28 @@
     else:
         rightward, leftward = (rank + 2) % dp, (rank + dp - 2) % dp
 
-        def mine(kind, k, to, core_of=core):
+        def mine(kind, k, to):
+            if kind == 4:
+                return h1.at[pl.ds(pl.multiple_of((k * line + to) * piece, 16), piece)]
             src, base = own_rows(kind)
-            return src.at[pl.ds(pl.multiple_of(base + (core_of * line + to) * piece, 16), piece), columns(kind, k)]
+            return src.at[pl.ds(pl.multiple_of(base + (core * line + to) * piece, 16), piece), columns(kind, k)]
 
         def crossing(kind, k, rows, size):
             ref, base = ((win, 0), (win, d // 2), (wout, 3 * d), (wout, 3 * d + d // 2))[kind]
             return ref.at[pl.ds(pl.multiple_of(base + rows, 16), size), columns(kind, k)]
 
         def from_left(kind, k, to):
-            ref, base = ((wout, 0), (wout, chunks * (line - 1)), (n2, 0), (n2, line - 1))[kind]
+            ref, base = ((wout, 0), (wout, chunks * (line - 1)), (n2, 0), (n2, line - 1), (sl1, 0))[kind]
             rows = (base + k * (line - 1) + to - 1) * piece
             return ref.at[pl.ds(pl.multiple_of(rows, 16), piece), pl.ds(0, widths[kind])]
 
         def from_right(kind, k, to):
-            ref, base = ((xin, 0), (u2, 0), (n2, 2 * (line - 1)), (n2, 3 * (line - 1)))[kind]
+            ref, base = ((xin, 0), (u2, 0), (n2, 2 * (line - 1)), (n2, 3 * (line - 1)), (sl1, shared * (line - 1)))[kind]
             rows = (base + k * (line - 1) + to) * piece
             return ref.at[pl.ds(pl.multiple_of(rows, 16), piece), pl.ds(0, widths[kind])]
 
         def sem_of(kind, k, to):
-            return (first_of[kind] + k) * line + to
+            return ((count if kind == 4 else first_of[kind]) + k) * line + to
 
         def cross_copy(kind, k):
             src, base = own_rows(kind)
@@ -682,6 +695,8 @@
             )
 
         def chip_sum(kind, k, to):
+            if kind == 4:
+                return mine(kind, k, to)[...].astype(F32)
             return mine(kind, k, to)[...].astype(F32) + crossing(kind, k, to * piece, piece)[...].astype(F32)
 
         def flow_right(kind, k):
@@ -723,8 +738,9 @@
         def out_stage(kind, k):
             if kind == 0:
                 return mid.at[pl.ds(pl.multiple_of(k * piece, 16), piece)]
-            if kind == 1:
-                return acc.at[pl.ds(pl.multiple_of(k * piece, 16), piece)]
+            if kind in (1, 4):
+                at = k + (chunks if kind == 4 else 0)
+                return acc.at[pl.ds(pl.multiple_of(at * piece, 16), piece)]
             return (tl, ts)[kind - 2]
 
         def out_copies(kind, k):
@@ -736,7 +752,7 @@
             return pltpu.make_async_copy(out_stage(kind, k), dst, outsem.at[c])
 
         def gather(kind, k):
-            width = (d, d, pl_, ps)[kind]
+            width = (d, d, pl_, ps, d)[kind]
             dst = out_stage(kind, k)
             dst[...] = chip_sum(kind, k, z)[:, 0:width]
 
@@ -750,7 +766,58 @@
                 left_copy(kind, k, z).wait_recv()
                 dst[...] += from_right(kind, k, z)[...].astype(F32)[:, 0:width]
 
-            out_copies(kind, k).start()
+            if kind == 4:
+                return_copy(k).start()
+            else:
+                out_copies(kind, k).start()
+
+        def lend_copy(k):
+            rows = pl.ds(pl.multiple_of(core * line * piece, 16), line * piece)
+            return pltpu.make_async_remote_copy(
+                src_ref=slope.at[rows, columns(0, k + 1)],
+                dst_ref=h1.at[pl.ds(pl.multiple_of(k * line * piece, 16), line * piece)],
+                send_sem=lent.at[0, k],
+                recv_sem=lent.at[1, k],
+                device_id={"section": partner},
+                device_id_type=MESH,
+            )
+
+        def return_copy(k):
+            return pltpu.make_async_remote_copy(
+                src_ref=out_stage(4, k),
+                dst_ref=out_stage(0, k + 1),
+                send_sem=lent.at[2, k],
+                recv_sem=lent.at[3, k],
+                device_id={"section": partner},
+                device_id_type=MESH,
+            )
+
+        def lend(c):
+            @pl.when(giver & (c >= 1) & (c <= shared))
+            def _():
+                @pl.when(c == 1)
+                def _():
+                    pl.semaphore_wait(ready.at[3], 1)
+
+                def one(to, carry):
+                    mine(0, c, to)[...] = chip_sum(0, c, to).astype(BF16)
+                    return carry
+
+                lax.fori_loop(0, line, one, 0)
+                lend_copy(c - 1).start()
+
+        def pair_copy(which):
+            return pltpu.make_async_copy(paired, (small_made, small_back)[which], pairs.at[which])
+
+        def pair(which):
+            if which:
+                pair_copy(0).wait()
+            src = (raw_a, raw_b)[which]
+            for r in range(0, ps, 32):
+                rows = slice(r, min(r + 32, ps))
+                images = [src[j, rows].astype(F32)[:, None, :] for j in range(n)]
+                paired[rows] = jnp.concatenate(images, axis=1).astype(BF16)
+            pair_copy(which).start()
 
         def vec_cross():
             return pltpu.make_async_remote_copy(
@@ -773,7 +840,35 @@
             )
 
         def first(kind, k):
+            if kind == 4:
+
+                @pl.when(k == 0)
+                def _():
+                    @pl.when(z < line - 1)
+                    def _():
+                        pl.semaphore_wait(ready.at[4], 1)
+
+                    @pl.when(z > 0)
+                    def _():
+                        pl.semaphore_wait(ready.at[5], 1)
+
+                lend_copy(k).wait_recv()
+                return
             product(kind, k)
+            if kind == 3:
+
+                @pl.when(taker)
+                def _():
+                    pl.semaphore_signal(ready.at[3], inc=1, device_id={"section": partner}, device_id_type=MESH)
+
+                    @pl.when(z > 0)
+                    def _():
+                        pl.semaphore_signal(ready.at[4], inc=1, device_id={"dp": leftward}, device_id_type=MESH)
+
+                    @pl.when(z < line - 1)
+                    def _():
+                        pl.semaphore_signal(ready.at[5], inc=1, device_id={"dp": rightward}, device_id_type=MESH)
+
             if kind == 0:
 
                 @pl.when(k == 0)
@@ -791,11 +886,15 @@
             cross_copy(kind, k).start()
 
         def crossed(kind, k):
-            cross_copy(kind, k).wait_recv()
+            if kind < 4:
+                cross_copy(kind, k).wait_recv()
 
         def finish(kind, k):
-            cross_copy(kind, k).wait_send()
-            out_copies(kind, k).wait()
+            if kind == 4:
+                return_copy(k).wait_send()
+            else:
+                cross_copy(kind, k).wait_send()
+                out_copies(kind, k).wait()
 
             def right(j, carry):
                 right_copy(kind, k, line - 1 - j).wait_send()
@@ -805,8 +904,13 @@
                 left_copy(kind, k, to).wait_send()
                 return carry
 
-            lax.fori_loop(0, line - 1 - z, right, 0)
-            lax.fori_loop(0, z, left, 0)
+            sent = line - 1 - z, z
+            if kind == 0:
+                away = giver & (k >= 1) & (k <= shared)
+                own_line = 1 - away.astype(jnp.int32)
+                sent = sent[0] * own_line, sent[1] * own_line
+            lax.fori_loop(0, sent[0], right, 0)
+            lax.fori_loop(0, sent[1], left, 0)
 
         pl.semaphore_signal(ready.at[0], inc=1, device_id={"dp": sibling}, device_id_type=MESH)
 
@@ -819,10 +923,10 @@
             pl.semaphore_signal(ready.at[2], inc=1, device_id={"dp": rightward}, device_id_type=MESH)
 
         def run(c, carry):
-
             ways(crossed)(c - 1)
-            ways(flow_right)(c - 1 - z, z < line - 1)
-            ways(flow_left)(c - line + z, z > 0)
+            lend(c - 1)
+            ways(flow_right, True)(c - 1 - z, z < line - 1)
+            ways(flow_left, True)(c - line + z, z > 0)
             ways(first)(c)
 
             @pl.when(c == count)
@@ -836,16 +940,31 @@
                 for k in range(1, line):
                     vec_copy(k).start()
 
-            ways(gather)(c - line - 1)
+            for which in range(2):
+
+                @pl.when(c == count - 2 + which)
+                def _(which=which):
+                    pair(which)
+
+            ways(gather, True)(c - line - 1)
             return carry
 
-        lax.fori_loop(0, count + line + 1, run, 0)
+        steps = count + 1 + shared
+        lax.fori_loop(0, steps + line + 1, run, 0)
+
+        @pl.when(giver)
+        def _():
+            for k in range(shared):
+                lend_copy(k).wait_send()
+                return_copy(k).wait_recv()
+                out_copies(0, k + 1).start()
 
         def end(c, carry):
             ways(finish)(c)
             return carry
 
-        lax.fori_loop(0, count, end, 0)
+        lax.fori_loop(0, steps, end, 0)
+        pair_copy(1).wait()
         for k in range(1, line):
             vec_copy(k).wait()
         value = vecs[0]
@@ -856,7 +975,8 @@
     for i in range(2 * n):
         unit = Unit(i < n, i % n)
         for b in range(unit.blocks):
-            unit.out_copy(1, b).wait()
+            if unit.large or not fused:
+                unit.out_copy(1, b).wait()
 
             @pl.when(place > 0)
             def _(b=b, unit=unit):
@@ -910,7 +1030,9 @@
     dp = lax.axis_size("dp")
     piece, tok_piece = d // dp, ds_ // dp
     fused = d % (16 * dp) == 0 and ds_ % (16 * dp) == 0 and dc == 4 * d and d == 2 * ds_ and 2 * dp * piece <= rows
-    dims = (sections, n, ps, pl_, pp, d, ds_, dc, dp, fused)
+    fused = fused and sections % 2 == 0 and sections > 2
+    shared = 2
+    dims = (sections, n, ps, pl_, pp, d, ds_, dc, dp, fused, shared)
     chunks = dc // d
     line = dp // 2 if fused else 1
     count = 2 * chunks + 2
@@ -963,14 +1085,17 @@
         pltpu.SemaphoreType.DMA((blocks,)),
         pltpu.SemaphoreType.DMA((blocks,)),
         pltpu.SemaphoreType.DMA((2, count)),
-        pltpu.SemaphoreType.DMA((2, count * line)),
-        pltpu.SemaphoreType.DMA((2, count * line)),
+        pltpu.SemaphoreType.DMA((2, (count + shared) * line)),
+        pltpu.SemaphoreType.DMA((2, (count + shared) * line)),
         pltpu.SemaphoreType.DMA((count,)),
         pltpu.SemaphoreType.DMA((2, line)),
-        pltpu.SemaphoreType.REGULAR((3,)),
+        pltpu.SemaphoreType.REGULAR((6,)),
+        pltpu.SemaphoreType.DMA((4, shared)),
         pltpu.VMEM((2 * tok_piece, pl_), F32),
         pltpu.VMEM((2 * tok_piece, ps), F32),
         pltpu.VMEM((line + 2, vec_rows, d), F32),
+        pltpu.VMEM((ps, n, d) if fused else (8, 128), BF16),
+        pltpu.SemaphoreType.DMA((2,)),
     ]
     if fused:
         reduced = (
@@ -986,10 +1111,11 @@
             jax.ShapeDtypeStruct((d, large_width), BF16),
             jax.ShapeDtypeStruct((d, small_width), BF16),
         )
+    small_shape = (ps, n, d) if fused else (n, ps, d)
     outs = (
-        jax.ShapeDtypeStruct((n, ps, d), BF16),
+        jax.ShapeDtypeStruct(small_shape, BF16),
         jax.ShapeDtypeStruct((n, pl_, d), BF16),
-        jax.ShapeDtypeStruct((n, ps, d), BF16),
+        jax.ShapeDtypeStruct(small_shape, BF16),
         jax.ShapeDtypeStruct((n, pl_, d), BF16),
         *reduced,
         jax.ShapeDtypeStruct((vec_rows, d), F32),
@@ -1042,6 +1168,7 @@
             in_specs=[vmem] * 3,
             out_specs=[vmem] * 12,
         )(tok_l, tok_s, vec)
+        made_s, back_s = (x.transpose(1, 0, 2) for x in (made_s, back_s))
     else:
         chan_a, chan_b = (lax.psum_scatter(x, "dp", scatter_dimension=0, tiled=True).astype(F32) for x in (chan_a, chan_b))
         tok = jnp.concatenate([tok_l, tok_s], axis=1).reshape(2, ds_, large_width + small_width)

time: 311 us -> 303 us (0.974)
  Pallas kernels: 296 us -> 288 us
    pallas_call x1, Pallas kernels: 294 us -> 287 us  [local(): pl.pallas_call(functools.partial(kernel, dims), out_shape=outs, in_specs=...]
where the time goes in v2:
time: 303 us; the launch traced here: 302 us
  Pallas kernels  288 us (95%)
  local copies, waits for them, and re-layouts  13.1 us (4%)
    pallas_call x1, Pallas kernels, local(): pl.pallas_call(functools.partial(kernel, dims), out_shape=outs, in_specs=...  287 us
    unnamed x14, local copies, waits for them, and re-layouts  10.7 us

profile of v2, /device:TPU:0, one launch (start us, length us, event | category | flops | bytes accessed | tf_op | source)
XLA Modules:
  0.0 302.2 jit_solution(2213320263600500591)
XLA Ops:
  0.7 2.4 copy_bitcast_fusion
  3.1 286.7 %shard_map.331 = (bf16[196,2,768]{2,1,0:T(2,128)(2,1)}, bf16[2,576,768]{2,1,0:T(8,128)(2,1)}, bf16[196,2,768]{2,1,0:T(2,128)(2,1)}, bf16[2,576,768]{2,1,0:T(8,12...) custom-call(bf16[2,196,768]{2,1,0:T(8,128)(2,1)} %get-tuple-element., ...), custom_call_target="tpu_custom_call" | custom-call | flops 49999998976 | bytes 40000000 | tf_op jit(solution)/shard_map/pallas_call | solution.py:1123
  289.8 1.7 shard_map.332
  291.5 2.3 copy.50
  293.8 0.0 copy-start.3
  293.8 0.0 copy-start
  293.8 2.9 copy.51
  296.8 0.0 copy-done.3
  296.8 0.8 copy.52
  297.6 0.0 copy-done
  297.6 0.0 copy-start.2
  297.6 1.2 copy.53
  298.8 0.7 copy-done.2
  299.5 0.0 copy-start.1
  299.5 1.0 copy.54
  300.5 0.7 copy-done.1
  301.2 1.0 copy.55
Async XLA Ops:
  293.8 3.0 copy-start.3
  293.8 3.8 %copy-start = (bf16[2,576,768]{2,1,0:T(8,128)(2,1)S(1)}, bf16[2,576,768]{2,1,0:T(8,128)(2,1)}, u32[]{:S(2)}) copy-start(bf16[2,576,768]{2,1,0:T(8,128)(2,1)} %get-tuple-element.42) | copy-start | bytes 5308420
  297.6 1.9 copy-start.2
  299.5 1.7 copy-start.1

commit v3 on v2

--- a/solution.py
+++ b/solution.py
@@ -134,7 +134,9 @@
     sibling = rank + 1 - 2 * core
     partner = (place + sections // 2) % sections
     giver = place < sections // 2
-    taker = place >= sections // 2
+    taker = place > 0
+    owner = (place + sections - 1) // 2 % 2
+    foreign = 1 + last
 
     def weight_copies():
         pairs = (
@@ -592,9 +594,9 @@
                 low, high = first_of[kind], first_of[kind] + kinds[kind]
                 here = (c >= low) & (c < high) & valid
                 if kind == 4:
-                    here = here & taker
+                    here = here & taker & (c < low + foreign)
                 if kind == 0 and kept:
-                    here = here & (taker | (c < 1) | (c > shared))
+                    here = here & ((place >= sections // 2) | (c < 1) | (c > shared))
 
                 @pl.when(here)
                 def _(kind=kind, low=low):
@@ -767,30 +769,36 @@
                 dst[...] += from_right(kind, k, z)[...].astype(F32)[:, 0:width]
 
             if kind == 4:
-                return_copy(k).start()
+                give_back(k).start()
             else:
                 out_copies(kind, k).start()
 
-        def lend_copy(k):
+        def lend_copy(j, f, to):
             rows = pl.ds(pl.multiple_of(core * line * piece, 16), line * piece)
             return pltpu.make_async_remote_copy(
-                src_ref=slope.at[rows, columns(0, k + 1)],
-                dst_ref=h1.at[pl.ds(pl.multiple_of(k * line * piece, 16), line * piece)],
-                send_sem=lent.at[0, k],
-                recv_sem=lent.at[1, k],
-                device_id={"section": partner},
+                src_ref=slope.at[rows, columns(0, j + 1)],
+                dst_ref=h1.at[pl.ds(pl.multiple_of(f * line * piece, 16), line * piece)],
+                send_sem=lent.at[0, j],
+                recv_sem=lent.at[1, f],
+                device_id={"section": to},
                 device_id_type=MESH,
             )
 
-        def return_copy(k):
+        def return_copy(f, j, to):
             return pltpu.make_async_remote_copy(
-                src_ref=out_stage(4, k),
-                dst_ref=out_stage(0, k + 1),
-                send_sem=lent.at[2, k],
-                recv_sem=lent.at[3, k],
-                device_id={"section": partner},
+                src_ref=out_stage(4, f),
+                dst_ref=out_stage(0, j + 1),
+                send_sem=lent.at[2, f],
+                recv_sem=lent.at[3, j],
+                device_id={"section": to},
                 device_id_type=MESH,
             )
+
+        def lend_away(j):
+            return lend_copy(j, place * j, (1 - place) * (2 - j) + place * 3)
+
+        def give_back(f):
+            return return_copy(f, f + (2 - place) * (1 - last), owner)
 
         def lend(c):
             @pl.when(giver & (c >= 1) & (c <= shared))
@@ -799,12 +807,16 @@
                 def _():
                     pl.semaphore_wait(ready.at[3], 1)
 
+                @pl.when((c == 2) & (place == 0))
+                def _():
+                    pl.semaphore_wait(ready.at[6], 1)
+
                 def one(to, carry):
                     mine(0, c, to)[...] = chip_sum(0, c, to).astype(BF16)
                     return carry
 
                 lax.fori_loop(0, line, one, 0)
-                lend_copy(c - 1).start()
+                lend_away(c - 1).start()
 
         def pair_copy(which):
             return pltpu.make_async_copy(paired, (small_made, small_back)[which], pairs.at[which])
@@ -852,14 +864,18 @@
                     def _():
                         pl.semaphore_wait(ready.at[5], 1)
 
-                lend_copy(k).wait_recv()
+                lend_copy(0, k, owner).wait_recv()
                 return
             product(kind, k)
             if kind == 3:
 
                 @pl.when(taker)
                 def _():
-                    pl.semaphore_signal(ready.at[3], inc=1, device_id={"section": partner}, device_id_type=MESH)
+                    for at, here in ((6, place == 1), (3, place > 1)):
+
+                        @pl.when(here)
+                        def _(at=at):
+                            pl.semaphore_signal(ready.at[at], inc=1, device_id={"section": owner}, device_id_type=MESH)
 
                     @pl.when(z > 0)
                     def _():
@@ -891,7 +907,7 @@
 
         def finish(kind, k):
             if kind == 4:
-                return_copy(k).wait_send()
+                give_back(k).wait_send()
             else:
                 cross_copy(kind, k).wait_send()
                 out_copies(kind, k).wait()
@@ -955,8 +971,8 @@
         @pl.when(giver)
         def _():
             for k in range(shared):
-                lend_copy(k).wait_send()
-                return_copy(k).wait_recv()
+                lend_away(k).wait_send()
+                return_copy(0, k, owner).wait_recv()
                 out_copies(0, k + 1).start()
 
         def end(c, carry):
@@ -983,7 +999,14 @@
                 behind_copy(unit.base + b * unit.size, unit.size, unit.slot + b).wait_send()
 
 
-def finish_kernel(tok_piece, d, chunks, tok_l, tok_s, vec, *outs):
+def finish_kernel(tok_piece, d, chunks, moved, *refs):
+    sources, (tok_l, tok_s, vec), rest = refs[:moved], refs[moved : moved + 3], refs[moved + 3 :]
+    outs, vias, sem = rest[: -moved - 1], rest[-moved - 1 : -1], rest[-1]
+    bring = [pltpu.make_async_copy(a, b, sem.at[0, k]) for k, (a, b) in enumerate(zip(sources, vias))]
+    take = [pltpu.make_async_copy(a, b, sem.at[1, k]) for k, (a, b) in enumerate(zip(vias, outs[:moved]))]
+    for c in bring:
+        c.start()
+    outs = outs[moved:]
     for k, src in enumerate((tok_l, tok_s)):
         outs[2 * k][...] = src[0:tok_piece]
         outs[2 * k + 1][...] = src[tok_piece:]
@@ -994,6 +1017,11 @@
         rows, width = out.shape
         out[...] = vec[at : at + rows, 0:width]
         at += rows
+    for a, b in zip(bring, take):
+        a.wait()
+        b.start()
+    for c in take:
+        c.wait()
 
 
 def local(
@@ -1030,7 +1058,7 @@
     dp = lax.axis_size("dp")
     piece, tok_piece = d // dp, ds_ // dp
     fused = d % (16 * dp) == 0 and ds_ % (16 * dp) == 0 and dc == 4 * d and d == 2 * ds_ and 2 * dp * piece <= rows
-    fused = fused and sections % 2 == 0 and sections > 2
+    fused = fused and sections == 4
     shared = 2
     dims = (sections, n, ps, pl_, pp, d, ds_, dc, dp, fused, shared)
     chunks = dc // d
@@ -1089,7 +1117,7 @@
         pltpu.SemaphoreType.DMA((2, (count + shared) * line)),
         pltpu.SemaphoreType.DMA((count,)),
         pltpu.SemaphoreType.DMA((2, line)),
-        pltpu.SemaphoreType.REGULAR((6,)),
+        pltpu.SemaphoreType.REGULAR((7,)),
         pltpu.SemaphoreType.DMA((4, shared)),
         pltpu.VMEM((2 * tok_piece, pl_), F32),
         pltpu.VMEM((2 * tok_piece, ps), F32),
@@ -1157,17 +1185,22 @@
         norm_shift[0],
     )
     if fused:
-        final = [jax.ShapeDtypeStruct((tok_piece, width), F32) for width in (pl_, pl_, ps, ps)]
+        large = (made_l, back_l, chan_a, chan_b, made_s, back_s)
+        final = [jax.ShapeDtypeStruct(x.shape, x.dtype) for x in large]
+        final += [jax.ShapeDtypeStruct((tok_piece, width), F32) for width in (pl_, pl_, ps, ps)]
         final += [
             jax.ShapeDtypeStruct(shape, F32)
             for shape in ((1, dc), (1, d), (2, d), (2, d), (1, ds_), (1, pl_), (1, ds_), (1, ps))
         ]
-        lin, lout, sin, sout, cbias, cshift, gain, shift, lbias, lshift, sbias, sshift = pl.pallas_call(
-            functools.partial(finish_kernel, tok_piece, d, chunks),
+        made_l, back_l, chan_a, chan_b, made_s, back_s, lin, lout, sin, sout, *vecs = pl.pallas_call(
+            functools.partial(finish_kernel, tok_piece, d, chunks, len(large)),
             out_shape=final,
-            in_specs=[vmem] * 3,
-            out_specs=[vmem] * 12,
-        )(tok_l, tok_s, vec)
+            in_specs=[any_] * len(large) + [vmem] * 3,
+            out_specs=[any_] * len(large) + [vmem] * 12,
+            scratch_shapes=[pltpu.VMEM(x.shape, x.dtype) for x in large] + [pltpu.SemaphoreType.DMA((2, len(large)))],
+            compiler_params=pltpu.CompilerParams(vmem_limit_bytes=65400 * 1024),
+        )(*large, tok_l, tok_s, vec)
+        cbias, cshift, gain, shift, lbias, lshift, sbias, sshift = vecs
         made_s, back_s = (x.transpose(1, 0, 2) for x in (made_s, back_s))
     else:
         chan_a, chan_b = (lax.psum_scatter(x, "dp", scatter_dimension=0, tiled=True).astype(F32) for x in (chan_a, chan_b))

time: 303 us -> 291 us (0.960)
  local copies, waits for them, and re-layouts: 13.1 us -> 2.4 us
    unnamed x14 -> x0, local copies, waits for them, and re-layouts: 10.7 us -> none
    pallas_call x1, Pallas kernels: 287 us -> 280 us  [local(): pl.pallas_call(functools.partial(kernel, dims), out_shape=outs, in_specs=...]
    pallas_call x1, Pallas kernels: 1.75 us -> 7.22 us  [local(): pl.pallas_call(functools.partial(finish_kernel, tok_piece, d, chunks, len...]
where the time goes in v3:
time: 291 us; the launch traced here: 290 us
  Pallas kernels  287 us (99%)
    pallas_call x1, Pallas kernels, local(): pl.pallas_call(functools.partial(kernel, dims), out_shape=outs, in_specs=...  280 us
    pallas_call x1, Pallas kernels, local(): pl.pallas_call(functools.partial(finish_kernel, tok_piece, d, chunks, len...  7.22 us

profile of v3, /device:TPU:0, one launch (start us, length us, event | category | flops | bytes accessed | tf_op | source)
XLA Modules:
  0.0 290.4 jit_solution(14847838143172303422)
XLA Ops:
  0.7 2.4 copy_bitcast_fusion
  3.1 279.9 %shard_map.331 = (bf16[196,2,768]{2,1,0:T(2,128)(2,1)}, bf16[2,576,768]{2,1,0:T(8,128)(2,1)}, bf16[196,2,768]{2,1,0:T(2,128)(2,1)}, bf16[2,576,768]{2,1,0:T(8,12...) custom-call(bf16[2,196,768]{2,1,0:T(8,128)(2,1)} %get-tuple-element., ...), custom_call_target="tpu_custom_call" | custom-call | flops 49999998976 | bytes 40000000 | tf_op jit(solution)/shard_map/pallas_call | solution.py:1151
  283.0 7.2 %shard_map.332 = (bf16[2,576,768]{2,1,0:T(8,128)(2,1)}, bf16[2,576,768]{2,1,0:T(8,128)(2,1)}, f32[96,3072]{1,0:T(8,128)}, f32[96,3072]{1,0:T(8,128)}, bf16[196,2...) custom-call(bf16[2,576,768]{2,1,0:T(8,128)(2,1)} %get-tuple-element., ...), custom_call_target="tpu_custom_call" | custom-call | tf_op jit(solution)/shard_map/pallas_call | solution.py:1195

commit v4 on v3

--- a/solution.py
+++ b/solution.py
@@ -189,7 +189,6 @@
             pl.semaphore_signal(barrier, inc=1, device_id={"dp": (rank + 2 * k) % dp}, device_id_type=MESH)
         pl.semaphore_signal(barrier, inc=1, device_id={"section": partner}, device_id_type=MESH)
         peers = peers + line + 1
-    pl.semaphore_wait(barrier, peers)
 
     def column(row, dst):
         width = up_to(dst.shape[0], 128)
@@ -214,9 +213,16 @@
             small_copy(small_images, raw_a, isem, j).start()
 
     lgin_t[...] = jnp.transpose(lgin[...])
-    lgout[...] = jnp.transpose(lgout_t[...])
     sgin_t[...] = jnp.transpose(sgin[...])
-    sgout[...] = jnp.transpose(sgout_t[...])
+
+    def prepare_backward():
+        lgout[...] = jnp.transpose(lgout_t[...])
+        sgout[...] = jnp.transpose(sgout_t[...])
+
+    @pl.when(last == 1)
+    def _():
+        prepare_backward()
+
 
     gains = norm_gain[...]
     shifts = norm_shift[...]
@@ -341,21 +347,30 @@
             rows = unit.at(b * size, size)
             here = slice(b * size, (b + 1) * size)
             total = channel_shift[...]
-            parts = [slice(c, c + WIDE) for c in range(0, dc, WIDE)]
+            parts = [slice(c, c + COLS) for c in range(0, dc, COLS)]
             ahead_of = mm(n2[rows], win[:, parts[0]], 1, 0)
+            acts = []
             for c, cols in enumerate(parts):
                 pre = ahead_of + channel_bias[:, cols]
                 if c + 1 < len(parts):
                     ahead_of = mm(n2[rows], win[:, parts[c + 1]], 1, 0)
                 act, slp = gelu_pair(pre)
-                act = act.astype(BF16)
-                hid[rows, cols] = act
+                acts.append(act.astype(BF16))
+                hid[rows, cols] = acts[-1]
                 slope[rows, cols] = slp.astype(BF16)
-                total = total + mm(act, wout[cols, :], 1, 0)
+                if cols.stop % WIDE == 0:
+                    total = total + mm(jnp.concatenate(acts, axis=1), wout[cols.stop - WIDE : cols.stop, :], 1, 0)
+                    acts = []
             y = (mid[here] + keep_two * total).astype(BF16)
             stage[rows] = y
             if not unit.large:
                 raw_a[unit.i] = y[0:ps]
+
+            if b == 0:
+
+                @pl.when(step == 0)
+                def _():
+                    pl.semaphore_wait(barrier, peers)
 
             @pl.when(place < sections - 1)
             def _(b=b, size=size):
@@ -394,17 +409,20 @@
 
             stage[rows] = up[rows] * keep_two.astype(BF16)
 
-            parts = [slice(c, c + WIDE) for c in range(0, dc, WIDE)]
+            parts = [slice(c, c + COLS) for c in range(0, dc, COLS)]
             total = None
             ahead_of = mm(stage[rows], wout[parts[0], :], 1, 1)
+            grads = []
             for c, cols in enumerate(parts):
                 grad = ahead_of
                 if c + 1 < len(parts):
                     ahead_of = mm(stage[rows], wout[parts[c + 1], :], 1, 1)
-                grad = (grad * slope[rows, cols].astype(F32)).astype(BF16)
-                slope[rows, cols] = grad
-                term = mm(grad, win[:, cols], 1, 1)
-                total = term if total is None else total + term
+                grads.append((grad * slope[rows, cols].astype(F32)).astype(BF16))
+                slope[rows, cols] = grads[-1]
+                if cols.stop % WIDE == 0:
+                    term = mm(jnp.concatenate(grads, axis=1), win[:, cols.stop - WIDE : cols.stop], 1, 1)
+                    total = term if total is None else total + term
+                    grads = []
             acc[here] = total
 
         def norm_two(r):
@@ -492,6 +510,10 @@
         back = (1 - last) * (t // units) + last * (t % 2)
         which = (1 - last) * (t % units) + last * (t // 2)
         small, i = unit_at(which)
+
+        @pl.when((t == units) & (last == 0))
+        def _():
+            prepare_backward()
 
         @pl.when(t == 2 * units - 1)
         def _():

time: 291 us -> 288 us (0.990)
  no operation moved by 1% of the time
where the time goes in v4:
time: 288 us
  Pallas kernels  285 us (99%)
    pallas_call x1, Pallas kernels, local(): pl.pallas_call(functools.partial(kernel, dims), out_shape=outs, in_specs=...  277 us
    pallas_call x1, Pallas kernels, local(): pl.pallas_call(functools.partial(finish_kernel, tok_piece, d, chunks, len...  7.22 us

profile of v4, /device:TPU:0, one launch (start us, length us, event | category | flops | bytes accessed | tf_op | source)
XLA Modules:
  0.0 287.8 jit_solution(6458556580518083147)
XLA Ops:
  0.7 2.4 copy_bitcast_fusion
  3.1 277.4 %shard_map.331 = (bf16[196,2,768]{2,1,0:T(2,128)(2,1)}, bf16[2,576,768]{2,1,0:T(8,128)(2,1)}, bf16[196,2,768]{2,1,0:T(2,128)(2,1)}, bf16[2,576,768]{2,1,0:T(8,12...) custom-call(bf16[2,196,768]{2,1,0:T(8,128)(2,1)} %get-tuple-element., ...), custom_call_target="tpu_custom_call" | custom-call | flops 49999998976 | bytes 40000000 | tf_op jit(solution)/shard_map/pallas_call | solution.py:1173
  280.5 7.2 %shard_map.332 = (bf16[2,576,768]{2,1,0:T(8,128)(2,1)}, bf16[2,576,768]{2,1,0:T(8,128)(2,1)}, f32[96,3072]{1,0:T(8,128)}, f32[96,3072]{1,0:T(8,128)}, bf16[196,2...) custom-call(bf16[2,576,768]{2,1,0:T(8,128)(2,1)} %get-tuple-element., ...), custom_call_target="tpu_custom_call" | custom-call | tf_op jit(solution)/shard_map/pallas_call | solution.py:1217

commit v5 on v4

--- a/solution.py
+++ b/solution.py
@@ -14,7 +14,7 @@
 DENSITY = 0.3989422804014327
 ROWS = 144
 COLS = 256
-WIDE = 512
+WIDE = 1024
 
 
 def up_to(value, step):
@@ -169,8 +169,11 @@
     def _():
         for i in range(n):
             large_copy(large_upstream, up, usem, i).start()
-        for j in range(n):
-            small_copy(small_upstream, raw_b, usem, j).start()
+        if fused:
+            pltpu.make_async_copy(small_upstream, paired, usem.at[n]).start()
+        else:
+            for j in range(n):
+                small_copy(small_upstream, raw_b, usem, j).start()
 
     barrier = pltpu.get_barrier_semaphore()
 
@@ -222,6 +225,14 @@
     @pl.when(last == 1)
     def _():
         prepare_backward()
+        if fused:
+            pltpu.make_async_copy(small_upstream, paired, usem.at[n]).wait()
+            for j in range(n):
+                base = first_rows + j * pp
+                up[base : base + pp] = jnp.zeros((pp, d), BF16)
+                for r in range(0, ps, 32):
+                    size = min(32, ps - r)
+                    up[base + r : base + r + size] = paired[r : r + size].astype(F32)[:, j, :].astype(BF16)
 
 
     gains = norm_gain[...]
@@ -384,7 +395,7 @@
         def _():
             if unit.large:
                 large_copy(large_upstream, up, usem, unit.i).wait()
-            else:
+            elif not fused:
                 small_copy(small_upstream, raw_b, usem, unit.i).wait()
                 up[unit.at(0, pp)] = jnp.zeros((pp, d), BF16)
                 up[unit.at(0, ps)] = raw_b[unit.i]
@@ -1187,7 +1198,7 @@
     )(
         small_images.reshape(n, ps, d),
         large_images.reshape(n, pl_, d),
-        small_upstream.reshape(n, ps, d),
+        small_upstream.reshape(n, ps, d).transpose(1, 0, 2) if fused else small_upstream.reshape(n, ps, d),
         large_upstream.reshape(n, pl_, d),
         small_keep.reshape(n, 2),
         large_keep.reshape(n, 2),

time: 288 us -> 288 us (level)
  no operation moved by 1% of the time
where the time goes in v5:
time: 288 us
  Pallas kernels  285 us (99%)
    pallas_call x1, Pallas kernels, local(): pl.pallas_call(functools.partial(kernel, dims), out_shape=outs, in_specs=...  278 us
    pallas_call x1, Pallas kernels, local(): pl.pallas_call(functools.partial(finish_kernel, tok_piece, d, chunks, len...  7.22 us

profile of v5, /device:TPU:0, one launch (start us, length us, event | category | flops | bytes accessed | tf_op | source)
XLA Modules:
  0.0 288.0 jit_solution(5578160412449637175)
XLA Ops:
  0.7 2.0 copy.42
  2.6 278.0 %shard_map.331 = (bf16[196,2,768]{2,1,0:T(2,128)(2,1)}, bf16[2,576,768]{2,1,0:T(8,128)(2,1)}, bf16[196,2,768]{2,1,0:T(2,128)(2,1)}, bf16[2,576,768]{2,1,0:T(8,12...) custom-call(bf16[2,196,768]{2,1,0:T(8,128)(2,1)} %bitcast.48, ...), custom_call_target="tpu_custom_call" | custom-call | flops 49999998976 | bytes 40000000 | tf_op jit(solution)/shard_map/pallas_call | solution.py:1184
  280.6 7.2 %shard_map.332 = (bf16[2,576,768]{2,1,0:T(8,128)(2,1)}, bf16[2,576,768]{2,1,0:T(8,128)(2,1)}, f32[96,3072]{1,0:T(8,128)}, f32[96,3072]{1,0:T(8,128)}, bf16[196,2...) custom-call(bf16[2,576,768]{2,1,0:T(8,128)(2,1)} %get-tuple-element., ...), custom_call_target="tpu_custom_call" | custom-call | tf_op jit(solution)/shard_map/pallas_call | solution.py:1228

commit v6 on v5

--- a/solution.py
+++ b/solution.py
@@ -629,7 +629,7 @@
                 if kind == 4:
                     here = here & taker & (c < low + foreign)
                 if kind == 0 and kept:
-                    here = here & ((place >= sections // 2) | (c < 1) | (c > shared))
+                    here = here & ((place >= sections // 2) | (c % 2 == 0))
 
                 @pl.when(here)
                 def _(kind=kind, low=low):
@@ -809,7 +809,7 @@
         def lend_copy(j, f, to):
             rows = pl.ds(pl.multiple_of(core * line * piece, 16), line * piece)
             return pltpu.make_async_remote_copy(
-                src_ref=slope.at[rows, columns(0, j + 1)],
+                src_ref=slope.at[rows, columns(0, 2 * j + 1)],
                 dst_ref=h1.at[pl.ds(pl.multiple_of(f * line * piece, 16), line * piece)],
                 send_sem=lent.at[0, j],
                 recv_sem=lent.at[1, f],
@@ -820,7 +820,7 @@
         def return_copy(f, j, to):
             return pltpu.make_async_remote_copy(
                 src_ref=out_stage(4, f),
-                dst_ref=out_stage(0, j + 1),
+                dst_ref=out_stage(0, 2 * j + 1),
                 send_sem=lent.at[2, f],
                 recv_sem=lent.at[3, j],
                 device_id={"section": to},
@@ -834,13 +834,13 @@
             return return_copy(f, f + (2 - place) * (1 - last), owner)
 
         def lend(c):
-            @pl.when(giver & (c >= 1) & (c <= shared))
+            @pl.when(giver & (c % 2 == 1) & (c >= 1) & (c < 2 * shared))
             def _():
                 @pl.when(c == 1)
                 def _():
                     pl.semaphore_wait(ready.at[3], 1)
 
-                @pl.when((c == 2) & (place == 0))
+                @pl.when((c == 3) & (place == 0))
                 def _():
                     pl.semaphore_wait(ready.at[6], 1)
 
@@ -849,7 +849,7 @@
                     return carry
 
                 lax.fori_loop(0, line, one, 0)
-                lend_away(c - 1).start()
+                lend_away(c // 2).start()
 
         def pair_copy(which):
             return pltpu.make_async_copy(paired, (small_made, small_back)[which], pairs.at[which])
@@ -955,7 +955,7 @@
 
             sent = line - 1 - z, z
             if kind == 0:
-                away = giver & (k >= 1) & (k <= shared)
+                away = giver & (k % 2 == 1)
                 own_line = 1 - away.astype(jnp.int32)
                 sent = sent[0] * own_line, sent[1] * own_line
             lax.fori_loop(0, sent[0], right, 0)
@@ -1006,7 +1006,7 @@
             for k in range(shared):
                 lend_away(k).wait_send()
                 return_copy(0, k, owner).wait_recv()
-                out_copies(0, k + 1).start()
+                out_copies(0, 2 * k + 1).start()
 
         def end(c, carry):
             ways(finish)(c)

time: 288 us -> 288 us (level)
  no operation moved by 1% of the time
where the time goes in v6:
time: 288 us
  Pallas kernels  285 us (99%)
    pallas_call x1, Pallas kernels, local(): pl.pallas_call(functools.partial(kernel, dims), out_shape=outs, in_specs=...  278 us
    pallas_call x1, Pallas kernels, local(): pl.pallas_call(functools.partial(finish_kernel, tok_piece, d, chunks, len...  7.22 us

profile of v6, /device:TPU:0, one launch (start us, length us, event | category | flops | bytes accessed | tf_op | source)
XLA Modules:
  0.0 287.6 jit_solution(4956246685485153695)
XLA Ops:
  0.7 2.0 copy.42
  2.6 277.6 %shard_map.331 = (bf16[196,2,768]{2,1,0:T(2,128)(2,1)}, bf16[2,576,768]{2,1,0:T(8,128)(2,1)}, bf16[196,2,768]{2,1,0:T(2,128)(2,1)}, bf16[2,576,768]{2,1,0:T(8,12...) custom-call(bf16[2,196,768]{2,1,0:T(8,128)(2,1)} %bitcast.48, ...), custom_call_target="tpu_custom_call" | custom-call | flops 49999998976 | bytes 40000000 | tf_op jit(solution)/shard_map/pallas_call | solution.py:1184
  280.2 7.2 %shard_map.332 = (bf16[2,576,768]{2,1,0:T(8,128)(2,1)}, bf16[2,576,768]{2,1,0:T(8,128)(2,1)}, f32[96,3072]{1,0:T(8,128)}, f32[96,3072]{1,0:T(8,128)}, bf16[196,2...) custom-call(bf16[2,576,768]{2,1,0:T(8,128)(2,1)} %get-tuple-element., ...), custom_call_target="tpu_custom_call" | custom-call | tf_op jit(solution)/shard_map/pallas_call | solution.py:1228
